TPU v7x, 32 devices: a whole 2x2x4 slice. The times are simulated.
32 devices in a mesh: dp: 8 (over z, x), narrow: 4 (over y, core).
Axes of the slice: x: 2, y: 2, z: 4, core: 2. Of those that a mesh axis runs over, the one named last changes fastest.
Arguments:
- tokens: bfloat16 [64, 512, 768], P(('dp', 'narrow')), may hold values from -6 to 6
- doc_lengths: int32 [64, 4], P(('dp', 'narrow')), may hold values from 1 to 256, 512 in all within a row
- cotangent: bfloat16 [64, 512, 768], P(('dp', 'narrow')), may hold values from -6 to 6
- qkv_weight: float32 [12, 192, 192], P(None, 'narrow', 'dp'), may hold values from -0.4375 to 0.4375
- out_weight: float32 [1, 768, 768], P(None, 'narrow', 'dp'), may hold values from -1.25 to 1.25
- ffn_in_weight: float32 [4, 768, 192], P(None, 'narrow', 'dp'), may hold values from -0.4375 to 0.4375
- ffn_out_weight: float32 [4, 768, 192], P(None, 'narrow', 'dp'), may hold values from -0.21875 to 0.21875
- vectors: float32 [12, 768], replicated, may hold values from -1.2 to 1.4, as said below
- qkv_moment: float32 [12, 192, 192], P(None, 'narrow', 'dp'), may hold values from -320 to 320
- out_moment: float32 [1, 768, 768], P(None, 'narrow', 'dp'), may hold values from -320 to 320
- ffn_in_moment: float32 [4, 768, 192], P(None, 'narrow', 'dp'), may hold values from -320 to 320
- ffn_out_moment: float32 [4, 768, 192], P(None, 'narrow', 'dp'), may hold values from -320 to 320
- vec_moment1: float32 [12, 768], replicated, may hold values from -64 to 64
- vec_moment2: float32 [12, 768], replicated, may hold values from 9.8304 to 39.3216
Outputs:
- out_act: bfloat16 [64, 512, 768], P(('dp', 'narrow'))
- grad_tokens: bfloat16 [64, 512, 768], P(('dp', 'narrow'))
- qkv_moment_new: float32 [12, 192, 192], P(None, 'narrow', 'dp')
- out_moment_new: float32 [1, 768, 768], P(None, 'narrow', 'dp')
- ffn_in_moment_new: float32 [4, 768, 192], P(None, 'narrow', 'dp')
- ffn_out_moment_new: float32 [4, 768, 192], P(None, 'narrow', 'dp')
- qkv_weight_new: float32 [12, 192, 192], P(None, 'narrow', 'dp')
- out_weight_new: float32 [1, 768, 768], P(None, 'narrow', 'dp')
- ffn_in_weight_new: float32 [4, 768, 192], P(None, 'narrow', 'dp')
- ffn_out_weight_new: float32 [4, 768, 192], P(None, 'narrow', 'dp')
- vec_moment1_new: float32 [12, 768], replicated
- vec_moment2_new: float32 [12, 768], replicated
- vectors_new: float32 [12, 768], replicated
Inputs may be any that keep to these rules, and one draw needn't show every extreme that they name: `vectors`: rows 0 and 2 lie near one, the other rows are spread around zero.
All inputs are finite; a program needn't handle non-finite values.
Results may differ from a plain program's by a relative error of at most 0.04.
Values may be sent and summed in bfloat16 or wider, within the bound.
A program may use at most 192 MiB of HBM per device.

v0:
```python
import functools
import math

import jax
import jax.numpy as jnp
from jax import lax
from jax.experimental import pallas as pl
from jax.experimental.pallas import tpu as pltpu
from jax.sharding import PartitionSpec as P

F32, BF16 = jnp.float32, jnp.bfloat16
MESH = pl.DeviceIdType.MESH
NORM_EPS = 1e-05
NS_STEPS = 5
STEP = 5
ns_first = 3.4445
ns_second = -4.775
ns_third = 2.0315
muon_rate = 0.5
muon_decay = 0.01
adam_rate = 0.4
VMEM = pl.BlockSpec(memory_space=pltpu.VMEM)


def nn(a, b):
    return lax.dot_general(a, b, (((1,), (0,)), ((), ())), preferred_element_type=F32)


def nt(a, b):
    return lax.dot_general(a, b, (((1,), (1,)), ((), ())), preferred_element_type=F32)


def tn(a, b):
    return lax.dot_general(a, b, (((0,), (0,)), ((), ())), preferred_element_type=F32)


def window(g):
    return 128 * (3 * (g // 2) + g % 2)


def join(parts):
    out = []
    for p in range(2):
        a, b = parts[2 * p], parts[2 * p + 1]
        out += [a[:, :128], a[:, 128:] + b[:, :128], b[:, 128:]]
    return jnp.concatenate(out, axis=1)


def ids(len_ref, row, shape, dim):
    pos = lax.broadcasted_iota(jnp.int32, shape, dim)
    out = jnp.zeros(shape, jnp.int32)
    end = jnp.int32(0)
    for j in range(4):
        end = end + len_ref[row, j]
        out = out + (pos >= end).astype(jnp.int32)
    return out


def hot(shape, row_at, col_at):
    rows = lax.broadcasted_iota(jnp.int32, shape, 0) + row_at
    cols = lax.broadcasted_iota(jnp.int32, shape, 1) + col_at
    return (rows == cols).astype(BF16)


def put_blocks(dst, base, value):
    for j in range(value.shape[1] // 128):
        dst[base + 192 * j : base + 192 * j + 192, :] = value[:, 128 * j : 128 * j + 128].astype(BF16)


def wide_rows(ref, base, count):
    parts = []
    for q in range(count):
        at = base + 1152 * q
        parts.append(jnp.concatenate([ref[at + 192 * j : at + 192 * j + 192, :] for j in range(6)], axis=1))
    return parts[0] if count == 1 else jnp.concatenate(parts, axis=0)


def gelu_parts(v):
    u = jnp.abs(v) * 0.7071067811865476
    den = 1.0 + 0.3275911 * u
    t = pl.reciprocal(den, approx=True)
    t = t * (2.0 - den * t)
    ex = jnp.exp(-u * u)
    poly = t * (0.254829592 + t * (-0.284496736 + t * (1.421413741 + t * (-1.453152027 + t * 1.061405429))))
    half = 0.5 * poly * ex
    cdf = jnp.where(v >= 0, 1.0 - half, half)
    return v * cdf, cdf + v * ex * 0.3989422804014327


def norm(h):
    mu = jnp.mean(h, axis=-1, keepdims=True)
    c = h - mu
    inv = lax.rsqrt(jnp.mean(c * c, axis=-1, keepdims=True) + NORM_EPS)
    return c * inv, inv


def norm_back(up, n, inv, gain):
    w = up * gain
    return inv * (w - jnp.mean(w, axis=-1, keepdims=True) - n * jnp.mean(w * n, axis=-1, keepdims=True))


def col_sum(v):
    return jnp.sum(v, axis=0, keepdims=True)


def turned(g):
    return 2 * (g % 2) + g // 2


def ffn_kernel(owned, x_ref, cot_ref, ct_ref, w1_ref, w2_ref, wo_ref, vec_ref, mo_ref, m1_ref, m2_ref,
               out_ref, res_ref, dct_ref, so_ref, s1_ref, s2_ref, gv_ref,
               fl_s, act_s, slope_s, db_s, g1_ref, g2_ref, go_ref):
    step = pl.program_id(0)
    T = x_ref.shape[1]
    vec = lambda i: vec_ref[i : i + 1, :]
    x = x_ref[0].astype(F32)
    ctx = ct_ref[0].T
    h1 = x + (nn(ctx, wo_ref[...]) + vec(6))
    n1, inv1 = norm(h1)
    first = n1 * vec(0) + vec(1)
    fl_s[...] = first.astype(BF16)
    branch = []
    for g in range(4):
        lo = window(g)
        inner = nn(fl_s[:, lo : lo + 256], w1_ref[g]) + vec(8 + g)
        a, sl = gelu_parts(inner)
        act_s[g] = a.astype(BF16)
        slope_s[g] = sl
        branch.append(nt(act_s[g], w2_ref[g]))
    h2 = first + (join(branch) + vec(7))
    n2, inv2 = norm(h2)
    out_ref[0] = (n2 * vec(2) + vec(3)).astype(BF16)
    dy = cot_ref[0].astype(F32)
    dh2 = norm_back(dy, n2, inv2, vec(2))
    dbl = dh2.astype(BF16)
    db_s[...] = dbl
    dbt = dbl.T
    flt = fl_s[...].T
    ones = jnp.ones((16, T), BF16)
    dfirst = []
    gb = []

    @pl.when(step == 0)
    def _():
        g1_ref[...] = jnp.zeros_like(g1_ref)
        g2_ref[...] = jnp.zeros_like(g2_ref)
        go_ref[...] = jnp.zeros_like(go_ref)
        gv_ref[...] = jnp.zeros_like(gv_ref)

    for g in range(4):
        lo = window(g)
        da = nn(db_s[:, lo : lo + 256], w2_ref[g])
        di = (da * slope_s[g]).astype(BF16)
        dfirst.append(nt(di, w1_ref[g]))
        g2_ref[g] += nn(dbt[192 * g : 192 * g + 192, :], act_s[g])
        ext = nn(jnp.concatenate([flt[192 * g : 192 * g + 192, :], ones], axis=0), di)
        g1_ref[g] += ext[:192]
        gb.append(ext[192:193])
    df = dh2 + join(dfirst)
    dh1 = norm_back(df, n1, inv1, vec(0))
    res_ref[0] = dh1
    dat = dh1.astype(BF16)
    go_ref[...] += nn(ct_ref[0], dat)
    dct_ref[0] = nt(wo_ref[...], dat).astype(BF16)
    z = jnp.zeros((1, x.shape[1]), F32)
    gv_ref[...] += jnp.concatenate(
        [col_sum(df * n1), col_sum(df), col_sum(dy * n2), col_sum(dy), z, z, col_sum(dat.astype(F32)), col_sum(dbl.astype(F32))] + gb, axis=0)


    @pl.when(step == pl.num_programs(0) - 1)
    def _():
        d, n = lax.axis_index("dp"), lax.axis_index("narrow")
        slim, wide = m1_ref.shape[1:]
        big = mo_ref.shape[2]
        sel_l = hot((wide, 768), n * wide, 0)
        sel_s = hot((192, slim), 0, d * slim)
        placed = nt(hot((768, big), 0, d * big), (0.95 * mo_ref[0]).astype(BF16)).astype(BF16)
        value = go_ref[...] + nn(placed, sel_l)
        for q in range(4):
            put_blocks(so_ref, 1152 * q, value[192 * q : 192 * q + 192])
        for dst, g_ref, m_ref in ((s1_ref, g1_ref, m1_ref), (s2_ref, g2_ref, m2_ref)):
            for g in range(4):
                placed = nn(sel_s, (0.95 * m_ref[g]).astype(BF16)).astype(BF16)
                value = g_ref[g] + nn(placed, sel_l)
                if owned:
                    put_blocks(dst, 576 * g, value[:, :384])
                    put_blocks(dst, 2304 + 576 * turned(g), value[:, 384:])
                else:
                    put_blocks(dst, 1152 * g, value)
        for dst in (so_ref, s1_ref, s2_ref):
            if dst.shape[0] > 4608:
                dst[4608:, :] = jnp.zeros((dst.shape[0] - 4608, 128), BF16)


def ffn(tokens, cot, ct, w1, w2, wo, vec, mo, m1, m2, rows, owned):
    n, seq, d = tokens.shape
    T = seq
    act = pl.BlockSpec((1, T, d), lambda i: (i, 0, 0))
    actt = pl.BlockSpec((1, d, T), lambda i: (i, 0, 0))
    full = lambda *s: pl.BlockSpec(s, lambda i: (0,) * len(s))
    return pl.pallas_call(
        functools.partial(ffn_kernel, owned),
        grid=(n,),
        out_shape=[
            jax.ShapeDtypeStruct((n, seq, d), BF16),
            jax.ShapeDtypeStruct((n, seq, d), F32),
            jax.ShapeDtypeStruct((n, d, seq), BF16),
        ]
        + [jax.ShapeDtypeStruct((rows, 128), BF16)] * 3
        + [jax.ShapeDtypeStruct((12, 768), F32)],
        in_specs=[act, act, actt, full(4, 256, 768), full(4, 256, 768), full(768, 768), full(12, 768), full(*mo.shape), full(*m1.shape), full(*m2.shape)],
        out_specs=[act, act, actt] + [full(rows, 128)] * 3 + [full(12, 768)],
        scratch_shapes=[
            pltpu.VMEM((T, d), BF16), pltpu.VMEM((4, T, 768), BF16), pltpu.VMEM((4, T, 768), F32), pltpu.VMEM((T, d), BF16),
            pltpu.VMEM((4, 192, 768), F32), pltpu.VMEM((4, 192, 768), F32), pltpu.VMEM((768, 768), F32),
        ],
        compiler_params=pltpu.CompilerParams(vmem_limit_bytes=60 * 2**20),
    )(tokens, cot, ct, w1, w2, wo, vec, mo, m1, m2)


class Place:
    def __init__(self, dp, narrow):
        self.X = 2 if dp % 2 == 0 else 1
        self.C = 2 if narrow % 2 == 0 else 1
        self.Z, self.Y = dp // self.X, narrow // self.C

    def locate(self):
        d, n = lax.axis_index("dp"), lax.axis_index("narrow")
        self.z, self.x = d // self.X, lax.rem(d, self.X)
        self.y, self.c = n // self.C, lax.rem(n, self.C)

    def count(self):
        return self.Z + self.X + self.Y + self.C - 4

    def at(self, axis, j):
        return lax.rem(getattr(self, axis) + j, getattr(self, axis.upper()))

    def device(self, axis, j):
        where = {a: getattr(self, a) for a in "zxyc"}
        where[axis] = self.at(axis, j)
        return (where["z"] * self.X + where["x"], where["y"] * self.C + where["c"])

    def other(self, dx, dy):
        return (self.z * self.X + lax.rem(self.x + dx, self.X), lax.rem(self.y + dy, self.Y) * self.C + self.c)

    def barrier(self, corner=False):
        sem = pltpu.get_barrier_semaphore()
        if corner:
            pl.semaphore_signal(sem, inc=1, device_id=self.other(1, 1), device_id_type=MESH)
        for axis in "zxyc":
            for j in range(1, getattr(self, axis.upper())):
                pl.semaphore_signal(sem, inc=1, device_id=self.device(axis, j), device_id_type=MESH)
        pl.semaphore_wait(sem, self.count() + int(corner))


class Wires:
    def __init__(self, place, send_sem, recv_sem):
        self.place, self.send_sem, self.recv_sem, self.makers = place, send_sem, recv_sem, []

    def plan(self, src, dst, axis, j):
        return self.plan_to(src, dst, lambda: self.place.device(axis, j))

    def plan_to(self, src, dst, device):
        k = len(self.makers)
        self.makers.append(
            lambda: pltpu.make_async_remote_copy(
                src_ref=src(),
                dst_ref=dst(),
                send_sem=self.send_sem.at[k],
                recv_sem=self.recv_sem.at[k],
                device_id=device(),
                device_id_type=MESH,
            )
        )
        return k

    def start(self, copies):
        for k in copies:
            self.makers[k]().start()

    def arrive(self, copies):
        for k in copies:
            self.makers[k]().wait_recv()

    def leave(self, copies):
        for k in copies:
            self.makers[k]().wait_send()

    def finish(self, skip=()):
        self.leave([k for k in range(len(self.makers)) if k not in skip])


def gather_copies(p):
    return (p.Z - 1) + p.Z * ((p.X - 1) + (p.Y - 1) + 2 * (p.X - 1) * (p.Y - 1) + (p.C - 1))


def gather_steps(p, wires, buf, half):
    z, x, y, c = p.z, p.x, p.y, p.c
    rest = buf.shape[4] - half

    def same(at):
        return (lambda: buf.at[at()],) * 2

    along, first, second, last = {}, {}, {}, {}
    for j in range(1, p.Z):
        along[j] = wires.plan(*same(lambda: (z, c, x, y)), "z", j)
    for i in range(p.Z):
        from_z = lambda i=i: p.at("z", p.Z - i) if i else z
        mine = lambda f=from_z: (f(), c, x, y)
        first[i] = [wires.plan(*same(mine), "x", j) for j in range(1, p.X)] + [wires.plan(*same(mine), "y", j) for j in range(1, p.Y)]
        second[i] = []
        for j in range(1, p.X):
            part = lambda f=from_z, j=j: (f(), c, p.at("x", p.X - j), y, pl.ds(0, half))
            second[i] += [wires.plan(*same(part), "y", q) for q in range(1, p.Y)]
        for j in range(1, p.Y):
            part = lambda f=from_z, j=j: (f(), c, x, p.at("y", p.Y - j), pl.ds(half, rest))
            second[i] += [wires.plan(*same(part), "x", q) for q in range(1, p.X)]
        last[i] = [wires.plan(*same(lambda f=from_z: (f(), c)), "c", j) for j in range(1, p.C)]

    def step(t):
        if t == 0:
            wires.start(along.values())
        if t < p.Z:
            if t:
                wires.arrive([along[t]])
            wires.start(first[t])
        if 1 <= t <= p.Z:
            wires.arrive(first[t - 1])
            wires.start(second[t - 1])
        if 2 <= t <= p.Z + 1:
            wires.arrive(second[t - 2])
            wires.start(last[t - 2])
        if t == p.Z + 2:
            for i in last:
                wires.arrive(last[i])

    return [functools.partial(step, t) for t in range(p.Z + 3)]


class Shares:
    def __init__(self, p, rows):
        cells = p.X * p.Y * p.Z
        unit = 16 * cells * p.C
        units = -(-rows // unit)
        self.a, self.b = 16 * ((units + 1) // 2), 16 * max(units // 2, 1)
        self.per_core = cells * (self.a + self.b)
        self.rows = p.C * self.per_core
        self.cells = cells
        self.copies = 2 * ((p.C - 1) + 2 * ((p.X - 1) + (p.Y - 1)) + 2 * (p.Z - 1))

    def scratch(self, p):
        a, b = self.a, self.b
        kinds = [
            (self.per_core,),
            (p.C - 1, self.per_core),
            (p.X - 1, p.Y * p.Z * a),
            (p.Y - 1, p.X * p.Z * b),
            (p.Y - 1, p.Z * a),
            (p.X - 1, p.Z * b),
            (p.Z - 1, a),
            (p.Z - 1, b),
        ]
        return [pltpu.VMEM(k + (128,), BF16) for k in kinds] + [pltpu.SemaphoreType.DMA((self.copies,))] * 2


def spread(start, size):
    return pl.ds(pl.multiple_of(start, 16), size)


def add_into(dst, at, parts):
    total = dst[at, :].astype(F32)
    for part in parts:
        total = total + part.astype(F32)
    dst[at, :] = total.astype(BF16)


def sum_steps(p, s, src, out, scratch):
    held, from_c, a1, b1, a2, b2, a3, b3, send_sem, recv_sem = scratch
    wires = Wires(p, send_sem, recv_sem)
    a, b, per = s.a, s.b, s.per_core
    ax, by = p.Y * p.Z * a, p.X * p.Z * b
    in_a = lambda x, y=0, z=0: ((x * p.Y + y) * p.Z + z) * a
    in_b = lambda y, x=0, z=0: s.cells * a + ((y * p.X + x) * p.Z + z) * b
    x, y, z, c = p.x, p.y, p.z, p.c
    base = c * per

    def cut(ref, start, size):
        return lambda: ref.at[spread(start(), size)]

    def both(start, size):
        return (cut(out, start, size),) * 2

    def slot(ref, j):
        return lambda: ref.at[j - 1]

    sends = [[] for _ in range(8)]
    for j in range(1, p.C):
        sends[0].append(wires.plan(cut(src, lambda j=j: p.at("c", j) * per, per), slot(from_c, j), "c", j))
        sends[7].append(wires.plan(*both(lambda: base, per), "c", j))
    for j in range(1, p.X):
        sends[1].append(wires.plan(cut(held, lambda j=j: in_a(p.at("x", j)), ax), slot(a1, j), "x", j))
        sends[2].append(wires.plan(cut(held, lambda j=j: in_b(y, p.at("x", j)), p.Z * b), slot(b2, j), "x", j))
        sends[5].append(wires.plan(*both(lambda: base + in_b(y, x), p.Z * b), "x", j))
        sends[6].append(wires.plan(*both(lambda: base + in_a(x), ax), "x", j))
    for j in range(1, p.Y):
        sends[1].append(wires.plan(cut(held, lambda j=j: in_b(p.at("y", j)), by), slot(b1, j), "y", j))
        sends[2].append(wires.plan(cut(held, lambda j=j: in_a(x, p.at("y", j)), p.Z * a), slot(a2, j), "y", j))
        sends[5].append(wires.plan(*both(lambda: base + in_a(x, y), p.Z * a), "y", j))
        sends[6].append(wires.plan(*both(lambda: base + in_b(y), by), "y", j))
    for j in range(1, p.Z):
        sends[3].append(wires.plan(cut(held, lambda j=j: in_a(x, y, p.at("z", j)), a), slot(a3, j), "z", j))
        sends[3].append(wires.plan(cut(held, lambda j=j: in_b(y, x, p.at("z", j)), b), slot(b3, j), "z", j))
        sends[4].append(wires.plan(*both(lambda: base + in_a(x, y, z), a), "z", j))
        sends[4].append(wires.plan(*both(lambda: base + in_b(y, x, z), b), "z", j))

    def total(ref, at, size, parts, count):
        value = ref[spread(at, size), :].astype(F32)
        for j in range(count):
            value = value + parts[j].astype(F32)
        return value.astype(BF16)

    def step(t):
        if t:
            wires.arrive(sends[t - 1])
        if t == 1:
            held[...] = total(src, base, per, from_c, p.C - 1)
        if t == 2:
            held[spread(in_a(x), ax), :] = total(held, in_a(x), ax, a1, p.X - 1)
            held[spread(in_b(y), by), :] = total(held, in_b(y), by, b1, p.Y - 1)
        if t == 3:
            held[spread(in_a(x, y), p.Z * a), :] = total(held, in_a(x, y), p.Z * a, a2, p.Y - 1)
            held[spread(in_b(y, x), p.Z * b), :] = total(held, in_b(y, x), p.Z * b, b2, p.X - 1)
        if t == 4:
            out[spread(base + in_a(x, y, z), a), :] = total(held, in_a(x, y, z), a, a3, p.Z - 1)
            out[spread(base + in_b(y, x, z), b), :] = total(held, in_b(y, x, z), b, b3, p.Z - 1)
        if t < 8:
            wires.start(sends[t])
        else:
            wires.finish()

    return [functools.partial(step, t) for t in range(9)]


def at_turn(turn, steps):
    for i, todo in enumerate(steps):
        if todo:

            @pl.when(turn == i)
            def _():
                for step in todo:
                    step()


def dealt(steps, turns):
    return [steps[len(steps) * i // turns : len(steps) * (i + 1) // turns] for i in range(turns)]


def fold(t, odd):
    rows, wide = t.shape
    if wide % 128 == 64:
        body = jnp.where(odd, t[:, 64:], t[:, : wide - 64])
        edge = jnp.where(odd, t[:, :64], t[:, wide - 64 :])
        a, b = edge[: rows // 2], edge[rows // 2 :]
        tiles = [body[:, 128 * j : 128 * j + 128] for j in range(wide // 128)]
        tiles.append(jnp.concatenate([jnp.where(odd, b, a), jnp.where(odd, a, b)], axis=1))
        return jnp.concatenate(tiles, axis=0)
    need = -(-wide // 128) * 128
    t = jnp.concatenate([t, jnp.zeros((rows, need - wide), t.dtype)], axis=1) if need > wide else t
    return jnp.concatenate([t[:, 128 * j : 128 * j + 128] for j in range(need // 128)], axis=0)


def fold_rows(rows, wide):
    return rows * (wide // 128) + rows // 2 if wide % 128 == 64 else rows * (-(-wide // 128))


def unfold(p, buf, base, rows, wide):
    out = []
    lane = lax.broadcasted_iota(jnp.int32, (rows // 2, 128), 1)
    size = fold_rows(rows, wide)
    for z in range(p.Z):
        for x in range(p.X):
            tiles = []
            for y in range(p.Y):
                got = [buf[z, c, x, y, base : base + size, :].astype(F32) for c in range(p.C)]
                if wide % 128 == 64:
                    k = wide // 128
                    even, odd = got
                    tiles += [even[rows * j : rows * j + rows] for j in range(k)]
                    e, o = even[rows * k :], odd[rows * k :]
                    top = jnp.where(lane < 64, e, o)
                    low = pltpu.roll(jnp.where(lane < 64, o, e), 64, 1)
                    tiles.append(jnp.concatenate([top, low], axis=0))
                    tiles += [odd[rows * j : rows * j + rows] for j in range(k)]
                else:
                    k = size // rows
                    for c in range(p.C):
                        t = jnp.concatenate([got[c][rows * j : rows * j + rows] for j in range(k)], axis=1).astype(BF16)
                        tiles.append(nn(t, hot((128 * k, 768), (y * p.C + c) * wide, 0)) if 128 * k == wide else nn(t, hot_cut((128 * k, 768), (y * p.C + c) * wide, wide)))
            if wide % 128 == 64:
                out.append(jnp.concatenate(tiles, axis=1))
            else:
                out.append(functools.reduce(lambda a, b: a + b, tiles))
    return out


def hot_cut(shape, at, limit):
    rows = lax.broadcasted_iota(jnp.int32, shape, 0)
    cols = lax.broadcasted_iota(jnp.int32, shape, 1)
    return jnp.logical_and(rows + at == cols, rows < limit).astype(BF16)


def open_kernel(p, len_ref, x_ref, wq_ref, wo_ref, w1_ref, w2_ref, vec_ref,
                qt_out, k_out, kt_out, v_out, ct_out, lse_ref, w1_out, w2_out, wo_out, wt_out,
                bufq, bufr, win_s, qt_s, k_s, kt_s, v_s, ct_s, vt_s, bias_s, vcol_s, send_q, recv_q, send_r, recv_r, out_sem):
    p.locate()
    n_rows, seq = x_ref.shape[:2]
    odd = lax.rem(lax.axis_index("narrow"), 2) == 1
    slim, tall = wq_ref.shape[1:]
    qrows = bufq.shape[4]
    for c in range(3):
        t = jnp.concatenate([wq_ref[4 * c + g] for g in range(4)], axis=0).T
        t = jnp.concatenate([t, jnp.zeros((tall, 128 - 4 * slim), F32)], axis=1)
        bufq[p.z, p.c, p.x, p.y, c * tall : c * tall + tall, :] = t.astype(BF16)
    if qrows > 3 * tall:
        bufq[p.z, p.c, p.x, p.y, 3 * tall :, :] = jnp.zeros((qrows - 3 * tall, 128), BF16)
    rows, wide = 4 * slim, 4 * tall
    size = fold_rows(rows, wide)
    big = wo_ref.shape[2]
    shards = [nt(hot((big, big), 0, 0), wo_ref[0].astype(BF16))]
    shards += [jnp.concatenate([r[g] for g in range(4)], axis=0) for r in (w1_ref, w2_ref)]
    folded = jnp.concatenate([fold(t, odd) for t in shards], axis=0)
    if bufr.shape[4] > 3 * size:
        folded = jnp.concatenate([folded, jnp.zeros((bufr.shape[4] - 3 * size, 128), F32)], axis=0)
    bufr[p.z, p.c, p.x, p.y] = folded.astype(BF16)
    p.barrier()
    wires_q, wires_r = Wires(p, send_q, recv_q), Wires(p, send_r, recv_r)
    steps_q = gather_steps(p, wires_q, bufq, qrows // 32 * 16)
    steps_r = gather_steps(p, wires_r, bufr, bufr.shape[4] // 32 * 16)
    for i, step in enumerate(steps_q):
        step()
        if i == 2:
            steps_r[0]()
    total = jnp.zeros((3 * 192, 1024), F32)
    dp = p.Z * p.X
    for pair in range(dp // 2):
        tiles = []
        for d in (2 * pair, 2 * pair + 1):
            z, x = d // p.X, d % p.X
            got = [bufq[z, c, x, y].astype(F32) for y in range(p.Y) for c in range(p.C)]
            tiles.append(jnp.concatenate([b[c * tall : c * tall + tall] for c in range(3) for b in got], axis=0))
        r = lax.broadcasted_iota(jnp.int32, (256, 1), 0)
        q = jnp.where(r < 128, r, r - 128)
        g = (q >= slim).astype(jnp.int32) + (q >= 2 * slim).astype(jnp.int32) + (q >= 3 * slim).astype(jnp.int32)
        col = 256 * g + jnp.where(jnp.logical_or(g == 1, g == 3), 64, 0) + jnp.where(r < 128, 2 * pair * slim, (2 * pair + 1) * slim) + q - g * slim
        col = jnp.where(q < 4 * slim, col, -1)
        place = (lax.broadcasted_iota(jnp.int32, (256, 1024), 1) == col).astype(BF16)
        total = total + nn(jnp.concatenate(tiles, axis=1).astype(BF16), place)
    win_s[...] = jnp.zeros_like(win_s)
    for g in range(4):
        off = 64 * (g % 2)
        stack = total[:, 256 * g : 256 * g + 256].astype(BF16)
        for c in range(3):
            win_s[c, g, off : off + 192, :] = stack[192 * c : 192 * c + 192]
        wt_out[g] = nt(hot((192, 256), off, 0), stack).astype(BF16)
    vcol_s[...] = vec_ref[0:8, :].T
    turns = dealt(steps_r[1:], 6 * n_rows)

    def out_copies(row, which=range(5)):
        pairs = ((qt_s, qt_out), (k_s, k_out), (kt_s, kt_out), (v_s, v_out), (ct_s, ct_out))
        return [pltpu.make_async_copy(pairs[i][0].at[row], pairs[i][1].at[row], out_sem.at[row, i]) for i in which]

    def one_row(row, carry):
        same = ids(len_ref, row, (seq, seq), 0) == ids(len_ref, row, (seq, seq), 1)
        bias_s[...] = jnp.where(same, 0.0, -1e30)
        for g in range(4):
            lo = window(g)
            xw = x_ref[row, :, lo : lo + 256]
            off = 64 * (g % 2)
            r = slice(192 * g, 192 * g + 192)
            q = nt(win_s[0, g, off : off + 192, :], xw) + vcol_s[r, 4:5]
            qt_s[row, r, :] = q.astype(BF16) * BF16(0.125)
            kt_s[row, r, :] = nt(win_s[1, g, off : off + 192, :], xw).astype(BF16)
            v = nt(win_s[2, g, off : off + 192, :], xw) + vcol_s[r, 5:6]
            vt_s[r, :] = v.astype(BF16)
        wide_of = lambda c: join([nt(x_ref[row, :, window(g) : window(g) + 256], win_s[c, g]) for g in range(4)])
        k_s[row] = wide_of(1).astype(BF16)
        v_s[row] = (wide_of(2) + vec_ref[5:6, :]).astype(BF16)
        for copy in out_copies(row, range(4)):
            copy.start()

        def pair(j, carry):
            lo = pl.multiple_of(128 * j, 128)
            kp = k_s[row, :, pl.ds(lo, 128)]
            for e in range(2):
                at = pl.ds(pl.multiple_of(lo + 64 * e, 64), 64)
                qh = qt_s[row, at, :]
                none = jnp.zeros_like(qh)
                s = nn(kp, jnp.concatenate([none, qh] if e else [qh, none], axis=0)) + bias_s[...]
                m = jnp.max(s, axis=0, keepdims=True)
                ex = jnp.exp(s - m)
                tot = jnp.sum(ex, axis=0, keepdims=True)
                ctx = nn(vt_s[at, :], ex.astype(BF16))
                ct_s[row, at, :] = (ctx * (1.0 / tot)).astype(BF16)
                lse_ref[row, pl.ds(2 * j + e, 1), :] = m + jnp.log(tot)
            at_turn(row * 6 + j, turns)
            return carry

        lax.fori_loop(0, 6, pair, 0)
        out_copies(row, (4,))[0].start()
        return carry

    lax.fori_loop(0, n_rows, one_row, 0)
    wires_q.finish()
    wires_r.finish()
    whole = unfold(p, bufr, 0, rows, wide)
    wo_out[...] = jnp.concatenate(whole, axis=0).astype(BF16)
    for i, dst in enumerate((w1_out, w2_out)):
        whole = unfold(p, bufr, (i + 1) * size, rows, wide)
        dst[...] = jnp.zeros_like(dst)
        for g in range(4):
            off = 64 * (g % 2)
            dst[g, off : off + 192, :] = jnp.concatenate([b[g * slim : g * slim + slim] for b in whole], axis=0).astype(BF16)
    for row in range(n_rows):
        for copy in out_copies(row):
            copy.wait()


def opening(p, lengths, tokens, wq, wo, w1, w2, vec, ident):
    n, seq, d = tokens.shape
    slim, tall = wq.shape[1:]
    up = lambda r, m: -(-r // m) * m
    qrows = up(3 * tall, 32)
    rrows = up(3 * fold_rows(4 * slim, 4 * tall), 32)
    count = gather_copies(p)
    hbm = pl.BlockSpec(memory_space=pl.ANY)
    act = lambda a, b: jax.ShapeDtypeStruct((n, a, b), BF16)
    return pl.pallas_call(
        functools.partial(open_kernel, p),
        out_shape=[act(d, seq), act(seq, d), act(d, seq), act(seq, d), act(d, seq), jax.ShapeDtypeStruct((n, 16, seq), F32)]
        + [jax.ShapeDtypeStruct((4, 256, 768), BF16)] * 2
        + [jax.ShapeDtypeStruct((768, 768), BF16), jax.ShapeDtypeStruct((4, 192, 576), BF16)],
        in_specs=[pl.BlockSpec(memory_space=pltpu.SMEM)] + [VMEM] * 6,
        out_specs=[hbm] * 5 + [VMEM] * 5,
        scratch_shapes=[
            pltpu.VMEM((p.Z, p.C, p.X, p.Y, qrows, 128), BF16),
            pltpu.VMEM((p.Z, p.C, p.X, p.Y, rrows, 128), BF16),
            pltpu.VMEM((3, 4, 256, 256), BF16),
            pltpu.VMEM((n, d, seq), BF16), pltpu.VMEM((n, seq, d), BF16), pltpu.VMEM((n, d, seq), BF16), pltpu.VMEM((n, seq, d), BF16), pltpu.VMEM((n, d, seq), BF16),
            pltpu.VMEM((d, seq), BF16), pltpu.VMEM((seq, seq), F32), pltpu.VMEM((d, 8), F32),
            pltpu.SemaphoreType.DMA((count,)), pltpu.SemaphoreType.DMA((count,)),
            pltpu.SemaphoreType.DMA((count,)), pltpu.SemaphoreType.DMA((count,)),
            pltpu.SemaphoreType.DMA((n, 5)),
        ],
        compiler_params=pltpu.CompilerParams(collective_id=ident, has_side_effects=True, vmem_limit_bytes=60 * 2**20),
    )(lengths, tokens, wq, wo, w1, w2, vec)


def on_diagonal(n):
    return lax.broadcasted_iota(jnp.int32, (n, n), 0) == lax.broadcasted_iota(jnp.int32, (n, n), 1)


def ns_start(values):
    return [y * (1.0 / (jnp.sqrt(jnp.sum(y * y)) + 1e-07)) for y in values]


def ns_poly(values):
    n = values[0].shape[0]
    diag = on_diagonal(n)
    lows = [y.astype(BF16) for y in values]
    grams = [nt(l, l) for l in lows]
    mids = [jnp.sum(jnp.where(diag, g, 0.0)) * (1.0 / n) for g in grams]
    rest = [jnp.where(diag, g - m, g) for g, m in zip(grams, mids)]
    lowr = [r.astype(BF16) for r in rest]
    squares = [nn(r, r) for r in lowr]
    return mids, [((ns_second + 2.0 * ns_third * m) * r + ns_third * s).astype(BF16) for m, r, s in zip(mids, rest, squares)]


def ns_step(values, mids, polys):
    moved = [nn(q, y.astype(BF16)) for q, y in zip(polys, values)]
    return [(ns_first + ns_second * m + ns_third * m * m) * y + t for m, y, t in zip(mids, values, moved)]


def close_kernel(p, shares, *refs):
    (len_ref, wt_ref, so_ref, s1_ref, s2_ref, gv_ref, gmq_ref, wq_ref, wo_ref, w1_ref, w2_ref, vec_ref, vm1_ref, vm2_ref,
     x_hbm, qt_hbm, k_hbm, kt_hbm, v_hbm, ct_hbm, lse_ref, dct_hbm, res_hbm,
     gt_ref, mq_ref, mo_ref, m1_ref, m2_ref, nq_ref, no_ref, n1_ref, n2_ref, f_ref, s_ref, v_ref,
     x_s, qt_s, k_s, kt_s, v_s, ct_s, dct_s, res_s, bias_s, dq_s, dk_s, dv_s, gq_s, gv2_s, sq_s, oo_s, o1_s, o2_s, oq_s,
     y_s, po_s, pf_s, mid_s, xo_s, xf_s, xq_s, xo_r, xf_r, xq_r, in_sem, x_send, x_recv) = refs[: 35 + 32]
    rest = refs[35 + 32 :]
    p.locate()
    d, n = lax.axis_index("dp"), lax.axis_index("narrow")
    n_rows, seq = x_s.shape[:2]
    pairs = ((qt_hbm, qt_s), (k_hbm, k_s), (dct_hbm, dct_s), (v_hbm, v_s), (ct_hbm, ct_s), (kt_hbm, kt_s), (x_hbm, x_s), (res_hbm, res_s))

    def loads(row):
        return [pltpu.make_async_copy(src.at[row], dst.at[row], in_sem.at[row, i]) for i, (src, dst) in enumerate(pairs)]

    for row in range(n_rows):
        for copy in loads(row):
            copy.start()
    p.barrier()
    sums = [sum_steps(p, s, src, out, rest[10 * i : 10 * i + 10])
            for i, (s, src, out) in enumerate(zip(shares, (so_ref, s1_ref, s2_ref, sq_s), (oo_s, o1_s, o2_s, oq_s)))]
    o, f1, f2, q = sums
    for step in (o[0], f1[0], f2[0]):
        step()
    turns = dealt([o[1], f1[1], o[2], f2[1], o[3], f1[2], o[4], f2[2], o[5], f1[3], o[6], f2[3], o[7], f1[4], f2[4]], 6 * n_rows)
    gq_s[...] = jnp.zeros_like(gq_s)
    gv2_s[...] = jnp.zeros_like(gv2_s)
    lane = lax.broadcasted_iota(jnp.int32, (192, 256), 1)

    def one_row(row, carry):
        same = ids(len_ref, row, (seq, seq), 0) == ids(len_ref, row, (seq, seq), 1)
        bias_s[...] = jnp.where(same, 0.0, -1e30)
        for copy in loads(row):
            copy.wait()

        def pair(j, carry):
            lo = pl.multiple_of(128 * j, 128)
            kp, vp = k_s[row, :, pl.ds(lo, 128)], v_s[row, :, pl.ds(lo, 128)]
            for e in range(2):
                at = pl.ds(pl.multiple_of(lo + 64 * e, 64), 64)
                qh, dc = qt_s[row, at, :], dct_s[row, at, :]
                none = jnp.zeros_like(qh)
                wide = lambda a: jnp.concatenate([none, a] if e else [a, none], axis=0)
                delta = jnp.sum(dc.astype(F32) * ct_s[row, at, :].astype(F32), axis=0, keepdims=True)
                s = nn(kp, wide(qh)) + bias_s[...]
                ex = jnp.exp(s - lse_ref[row, pl.ds(2 * j + e, 1), :])
                de = nn(vp, wide(dc))
                ds = (ex * (de - delta)).astype(BF16)
                dv_s[at, :] = nt(dc, ex.astype(BF16)).astype(BF16)
                dk_s[at, :] = nt(qh, ds).astype(BF16)
                dq_s[at, :] = (nn(kt_s[row, at, :], ds) * 0.125).astype(BF16)
            at_turn(row * 6 + j, turns)
            return carry

        lax.fori_loop(0, 6, pair, 0)
        dx = []
        for g in range(4):
            lo = window(g)
            r = slice(192 * g, 192 * g + 192)
            cat = jnp.concatenate([dq_s[r, :], dk_s[r, :], dv_s[r, :]], axis=0)
            dx.append(nn(wt_ref[g], cat))
            gq = nn(cat, x_s[row, :, lo : lo + 256])
            keep = (lane < 192) if g % 2 == 0 else (lane >= 64)
            for c in range(3):
                gq_s[c, :, lo : lo + 256] += jnp.where(keep, gq[192 * c : 192 * c + 192], 0.0)
        gt_ref[row] = (res_s[row] + jnp.concatenate(dx, axis=0).T).astype(BF16)
        ones = jnp.ones((16, seq), BF16)
        gv2_s[0:1, :] += nt(ones, dq_s[...])[0:1]
        gv2_s[1:2, :] += nt(ones, dv_s[...])[0:1]
        return carry

    lax.fori_loop(0, n_rows, one_row, 0)
    slim, tall = gmq_ref.shape[1:]
    up = hot((192, tall), 0, n * tall)
    for c in range(3):
        held = jnp.zeros((tall, 768), F32)
        for g in range(4):
            held = held + tn((0.95 * gmq_ref[4 * c + g]).astype(BF16), hot((slim, 768), 192 * g + d * slim, 0))
        put_blocks(sq_s, 1152 * c, gq_s[c] + nn(up, held.astype(BF16)))
    gv = jnp.concatenate([gv_ref[0:4], gv2_s[0:2], gv_ref[6:12]], axis=0)
    tail = sq_s.shape[0] - 3456
    flat = jnp.concatenate([gv[:, 128 * j : 128 * j + 128] for j in range(6)] + [jnp.zeros((tail - 72, 128), F32)], axis=0)
    sq_s[3456:, :] = flat.astype(BF16)
    for step in (q[0], o[8], q[1]):
        step()
    wide, cols = w1_ref.shape[2], w1_ref.shape[1]
    sel_l = hot((wide, 768), n * wide, 0)
    sel_s = hot((cols, 192), d * cols, 0)
    big = wo_ref.shape[2]
    sel_b = hot((big, 768), d * big, 0)
    core0, core1 = p.c == 0, p.c == 1
    eight = lambda: [y_s[192 * i : 192 * i + 192, :] for i in range(8)]

    late = 3
    before = [[f1[5]], [f1[6]], [f1[7]], [q[5]], [q[7]]]
    between = [[q[2], f2[5]], [q[3], f2[6]], [q[4], f2[7], f1[8], f2[8]], [q[6]], [q[8]]]

    def sweep(t, carry):
        on0 = jnp.logical_and(core0, t < NS_STEPS)
        on1 = jnp.logical_and(core1, t >= late)

        @pl.when(jnp.logical_and(core0, t == 0))
        def _():
            y_s[0:768, :] = ns_start([wide_rows(oo_s, 0, 4).astype(F32)])[0]

        @pl.when(jnp.logical_and(core1, t == late))
        def _():
            for i, y in enumerate(ns_start([wide_rows(r, 1152 * g, 1).astype(F32) for r in (o1_s, o2_s) for g in range(4)])):
                y_s[192 * i : 192 * i + 192, :] = y

        @pl.when(on0)
        def _():
            mids, polys = ns_poly([y_s[0:768, :]])
            mid_s[0:1, :] = jnp.broadcast_to(mids[0], (1, 128))
            po_s[...] = polys[0]

        @pl.when(on1)
        def _():
            mids, polys = ns_poly(eight())
            for i in range(8):
                mid_s[i : i + 1, :] = jnp.broadcast_to(mids[i], (1, 128))
                pf_s[i] = polys[i]

        at_turn(t, before)

        @pl.when(on0)
        def _():
            y_s[0:768, :] = ns_step([y_s[0:768, :]], [mid_s[0:1, 0:1]], [po_s[...]])[0]

        @pl.when(on1)
        def _():
            for i, y in enumerate(ns_step(eight(), [mid_s[i : i + 1, 0:1] for i in range(8)], [pf_s[i] for i in range(8)])):
                y_s[192 * i : 192 * i + 192, :] = y

        at_turn(t, between)
        return carry

    lax.fori_loop(0, NS_STEPS + late, sweep, 0)
    wires = Wires(p, x_send, x_recv)
    mo_ref[0] = nt(sel_l, nn(sel_b, wide_rows(oo_s, 0, 4)).astype(BF16))
    for ref, m_ref in ((o1_s, m1_ref), (o2_s, m2_ref)):
        for g in range(4):
            m_ref[g] = nt(nn(sel_s, wide_rows(ref, 1152 * g, 1)).astype(BF16), sel_l)

    @pl.when(core0)
    def _():
        xo_s[...] = nn(sel_b, y_s[0:768, :].astype(BF16)).astype(BF16)

    @pl.when(core1)
    def _():
        for i in range(8):
            xf_s[cols * i : cols * i + cols, :] = nn(sel_s, y_s[192 * i : 192 * i + 192, :].astype(BF16)).astype(BF16)

    rows = [wide_rows(oq_s, 1152 * c, 1) for c in range(3)]
    spot = lambda g: hot_cut((256, 128), 0, 0)

    def square(parity):
        keep = (lane < 192) if parity == 0 else (lane >= 64)
        which = [(c, g) for c in range(3) for g in (parity, parity + 2)]
        ys = ns_start([jnp.where(keep, rows[c][:, window(g) : window(g) + 256].astype(F32), 0.0) for c, g in which])
        for i, y in enumerate(ys):
            y_s[192 * i : 192 * i + 192, :256] = y

        def turn(t, carry):
            ys = [y_s[192 * i : 192 * i + 192, :256] for i in range(6)]
            for i, y in enumerate(ns_step(ys, *ns_poly(ys))):
                y_s[192 * i : 192 * i + 192, :256] = y
            return carry

        lax.fori_loop(0, NS_STEPS, turn, 0)
        ys = [y_s[192 * i : 192 * i + 192, :256] for i in range(6)]
        for c in range(3):
            part = jnp.zeros((192, 128), F32)
            for (cc, g), y in zip(which, ys):
                if cc == c:
                    at = 64 * (g % 2) + d * slim
                    r = lax.broadcasted_iota(jnp.int32, (256, 128), 0) - at
                    q = lax.broadcasted_iota(jnp.int32, (256, 128), 1) - g * slim
                    sel = jnp.logical_and(r == q, jnp.logical_and(q >= 0, q < slim)).astype(BF16)
                    part = part + nn(y.astype(BF16), sel)
            xq_s[192 * c : 192 * c + 192, :] = part.astype(BF16)

    @pl.when(core0)
    def _():
        square(0)

    @pl.when(core1)
    def _():
        square(1)

    copies = [wires.plan(lambda a=a: a, lambda b=b: b, "c", 1) for a, b in ((xq_s, xq_r), (xo_s, xo_r), (xf_s, xf_r))]
    wires.start(copies)
    sel_o = hot((tall, 192), n * tall, 0)
    for c in range(3):
        mine = nn(sel_o, rows[c]).astype(BF16)
        for g in range(4):
            mq_ref[4 * c + g] = nt(hot((slim, 768), 192 * g + d * slim, 0), mine)
    vt = oq_s[3456 : 3456 + 80, :].astype(F32)
    grad = jnp.concatenate([vt[12 * j : 12 * j + 12] for j in range(6)], axis=1)
    first = 0.9 * vm1_ref[...] + 0.1 * grad
    second = 0.999 * vm2_ref[...] + 0.001 * grad * grad
    f_ref[...] = first
    s_ref[...] = second
    v_ref[...] = vec_ref[...] - adam_rate * (first * (1.0 / (1.0 - 0.9**STEP))) / (jnp.sqrt(second * (1.0 / (1.0 - 0.999**STEP))) + 1e-08)

    def fresh(w, own, longest):
        return w - muon_rate * (0.2 * math.sqrt(longest) * own + muon_decay * w)

    wires.arrive(copies)
    for c in range(3):
        both = (xq_s[192 * c : 192 * c + 192, :].astype(F32) + xq_r[192 * c : 192 * c + 192, :].astype(F32)).astype(BF16)
        mine = nn(sel_o, both).astype(BF16)
        for g in range(4):
            nq_ref[4 * c + g] = fresh(wq_ref[4 * c + g], nt(hot((slim, 128), g * slim, 0), mine), 192)
    xo = jnp.where(core0, xo_s[...], xo_r[...])
    no_ref[0] = fresh(wo_ref[0], nt(sel_l, xo), 768)
    for i, (w_ref, n_ref) in enumerate(((w1_ref, n1_ref), (w2_ref, n2_ref))):
        for g in range(4):
            at = slice(cols * (4 * i + g), cols * (4 * i + g) + cols)
            n_ref[g] = fresh(w_ref[g], nt(jnp.where(core1, xf_s[at, :], xf_r[at, :]), sel_l), 768)
    wires.finish()


def closing(p, shares, lengths, wt, so, s1, s2, gv, mq, weights, vec, vm1, vm2, acts, ident):
    tokens, lse = acts[0], acts[6]
    n, seq, d = tokens.shape
    slim = mq.shape[1]
    shape = lambda a: jax.ShapeDtypeStruct(a.shape, F32)
    outs = [jax.ShapeDtypeStruct(tokens.shape, BF16)] + [shape(w) for w in weights] * 2 + [shape(vec)] * 3
    hbm = pl.BlockSpec(memory_space=pl.ANY)
    tm, mt = pltpu.VMEM((n, seq, d), BF16), pltpu.VMEM((n, d, seq), BF16)
    flat = lambda r: pltpu.VMEM((r, 128), BF16)
    scratch = [tm, mt, tm, mt, tm, mt, mt, pltpu.VMEM((n, seq, d), F32), pltpu.VMEM((seq, seq), F32)]
    scratch += [pltpu.VMEM((d, seq), BF16)] * 3 + [pltpu.VMEM((3, 192, 768), F32), pltpu.VMEM((8, 768), F32)]
    scratch += [flat(shares[3].rows)] + [flat(s.rows) for s in shares]
    scratch += [pltpu.VMEM((1536, 768), F32), pltpu.VMEM((768, 768), BF16), pltpu.VMEM((8, 192, 192), BF16), pltpu.VMEM((8, 128), F32)]
    scratch += [pltpu.VMEM((4 * slim, 768), BF16), pltpu.VMEM((8 * slim, 768), BF16), pltpu.VMEM((576, 128), BF16)] * 2
    scratch += [pltpu.SemaphoreType.DMA((n, 8)), pltpu.SemaphoreType.DMA((3,)), pltpu.SemaphoreType.DMA((3,))]
    for s in shares:
        scratch += s.scratch(p)
    return pl.pallas_call(
        functools.partial(close_kernel, p, shares),
        out_shape=outs,
        in_specs=[pl.BlockSpec(memory_space=pltpu.SMEM)] + [VMEM] * 13 + [hbm] * 6 + [VMEM] + [hbm] * 2,
        out_specs=[VMEM] * 12,
        scratch_shapes=scratch,
        compiler_params=pltpu.CompilerParams(collective_id=ident, has_side_effects=True, vmem_limit_bytes=62 * 2**20),
    )(lengths, wt, so, s1, s2, gv, mq, *weights, vec, vm1, vm2, *acts)


class Owned:
    def __init__(self, p, half):
        self.half, self.rows, self.copies = half, 8 * half, 4 + 2 * (p.Z - 1)
        self.kinds = [4 * half, 4 * half, 2 * half, half, (p.Z - 1) * (half // p.Z), half, half]

    def scratch(self):
        return [pltpu.VMEM((k, 128), BF16) for k in self.kinds] + [pltpu.SemaphoreType.DMA((self.copies,))] * 2


def owned_steps(p, s, src, scratch):
    held, from_c, r1, r2, r3, mine, other, send_sem, recv_sem = scratch
    wires = Wires(p, send_sem, recv_sem)
    h, q, z, c = s.half, s.half // p.Z, p.z, p.c
    first = jnp.where(c == 0, p.x, p.y)
    second = jnp.where(c == 0, p.y, p.x)
    cut = lambda ref, start, size: lambda: ref.at[spread(start(), size)]

    def partner(turn):
        along_x = c == turn
        x, y = jnp.where(along_x, 1 - p.x, p.x), jnp.where(along_x, p.y, 1 - p.y)
        return (z * p.X + x, y * p.C + c)

    sibling = lambda: p.device("c", 1)
    spot = lambda: (2 * first + second) * h
    sends = [
        [wires.plan_to(cut(src, lambda: (1 - c) * 4 * h, 4 * h), lambda: from_c, sibling)],
        [wires.plan_to(cut(held, lambda: (1 - first) * 2 * h, 2 * h), lambda: r1, lambda: partner(0))],
        [wires.plan_to(cut(held, lambda: (2 * first + 1 - second) * h, h), lambda: r2, lambda: partner(1))],
        [],
        [],
        [wires.plan_to(lambda: mine, lambda: other, sibling)],
    ]
    for j in range(1, p.Z):
        sends[3].append(wires.plan(cut(held, lambda j=j: spot() + p.at("z", j) * q, q), lambda j=j: r3.at[pl.ds((j - 1) * q, q)], "z", j))
        sends[4].append(wires.plan(*(cut(mine, lambda: z * q, q),) * 2, "z", j))

    def add(dst, to, ref, start, size, parts):
        value = ref[spread(start, size), :].astype(F32)
        for part in parts:
            value = value + part().astype(F32)
        dst[spread(to, size), :] = value.astype(BF16)

    def step(t):
        if 1 <= t <= 5:
            wires.arrive(sends[t - 1])
        if t == 1:
            add(held, 0, src, c * 4 * h, 4 * h, [lambda: from_c[...]])
        if t == 2:
            add(held, first * 2 * h, held, first * 2 * h, 2 * h, [lambda: r1[...]])
        if t == 3:
            add(held, spot(), held, spot(), h, [lambda: r2[...]])
        if t == 4:
            add(mine, z * q, held, spot() + z * q, q, [lambda j=j: r3[(j - 1) * q : j * q, :] for j in range(1, p.Z)])
        if t < 5:
            wires.start(sends[t])
        if t == 5:

            @pl.when(c == 0)
            def _():
                wires.start(sends[5])

        if t == 6:
            wires.finish(skip=sends[5])

            @pl.when(c == 0)
            def _():
                wires.leave(sends[5])

            @pl.when(c == 1)
            def _():
                wires.arrive(sends[5])

    return [functools.partial(step, t) for t in range(7)]


def canon(odd, base):
    r = lax.broadcasted_iota(jnp.int32, (256, 128), 0)
    s = lax.broadcasted_iota(jnp.int32, (256, 128), 1)
    channel = jnp.where(odd, jnp.where(r < 128, r + 64, r - 128), r)
    return jnp.where(r < 192, channel - base, -1000), s


def owner_kernel(p, shares, *refs):
    (len_ref, wt_ref, so_ref, s1_ref, s2_ref, gv_ref, gmq_ref, wq_ref, wo_ref, w1_ref, w2_ref, vec_ref, vm1_ref, vm2_ref,
     x_hbm, qt_hbm, k_hbm, kt_hbm, v_hbm, ct_hbm, lse_ref, dct_hbm, res_hbm,
     gt_ref, mq_ref, mo_ref, m1_ref, m2_ref, nq_ref, no_ref, n1_ref, n2_ref, f_ref, s_ref, v_ref,
     x_s, qt_s, k_s, kt_s, v_s, ct_s, dct_s, res_s, bias_s, dq_s, dk_s, dv_s, gq_s, gv2_s, sq_s, oo_s,
     yo_s, po_s, yf_s, yq_s, mid_s, pf_s, xo_s, xo_r, tmf_s, txf_s, tmq_s, txq_s, tv_s, rmf_s, rxf_s, rmq_s, rxq_s, rv_s,
     in_sem, x_send, x_recv) = refs[: 35 + 37]
    rest = refs[35 + 37 :]
    p.locate()
    d, n = lax.axis_index("dp"), lax.axis_index("narrow")
    core0, core1 = p.c == 0, p.c == 1
    n_rows, seq = x_s.shape[:2]
    pairs = ((qt_hbm, qt_s), (k_hbm, k_s), (dct_hbm, dct_s), (v_hbm, v_s), (ct_hbm, ct_s), (kt_hbm, kt_s), (x_hbm, x_s), (res_hbm, res_s))

    def loads(row):
        return [pltpu.make_async_copy(src.at[row], dst.at[row], in_sem.at[row, i]) for i, (src, dst) in enumerate(pairs)]

    for row in range(n_rows):
        for copy in loads(row):
            copy.start()
    p.barrier(corner=True)
    o = sum_steps(p, shares[0], so_ref, oo_s, rest[:10])
    f1 = owned_steps(p, shares[1], s1_ref, rest[10:19])
    f2 = owned_steps(p, shares[2], s2_ref, rest[19:28])
    q = owned_steps(p, shares[3], sq_s, rest[28:37])
    f1_half, f1_other, f2_half, f2_other, q_half, q_other = rest[15], rest[16], rest[24], rest[25], rest[33], rest[34]
    for step in (o[0], f1[0], f2[0]):
        step()
    turns = dealt([o[1], f1[1], o[2], f2[1], o[3], f1[2], o[4], f2[2], f1[3], o[5], f2[3], o[6], f1[4], o[7], f2[4], f1[5], f2[5], o[8]], 6 * n_rows)
    gq_s[...] = jnp.zeros_like(gq_s)
    gv2_s[...] = jnp.zeros_like(gv2_s)
    lane = lax.broadcasted_iota(jnp.int32, (192, 256), 1)

    def one_row(row, carry):
        same = ids(len_ref, row, (seq, seq), 0) == ids(len_ref, row, (seq, seq), 1)
        bias_s[...] = jnp.where(same, 0.0, -1e30)
        for copy in loads(row):
            copy.wait()

        def pair(j, carry):
            lo = pl.multiple_of(128 * j, 128)
            kp, vp = k_s[row, :, pl.ds(lo, 128)], v_s[row, :, pl.ds(lo, 128)]
            for e in range(2):
                at = pl.ds(pl.multiple_of(lo + 64 * e, 64), 64)
                qh, dc = qt_s[row, at, :], dct_s[row, at, :]
                none = jnp.zeros_like(qh)
                wide = lambda a: jnp.concatenate([none, a] if e else [a, none], axis=0)
                delta = jnp.sum(dc.astype(F32) * ct_s[row, at, :].astype(F32), axis=0, keepdims=True)
                s = nn(kp, wide(qh)) + bias_s[...]
                ex = jnp.exp(s - lse_ref[row, pl.ds(2 * j + e, 1), :])
                de = nn(vp, wide(dc))
                ds = (ex * (de - delta)).astype(BF16)
                dv_s[at, :] = nt(dc, ex.astype(BF16)).astype(BF16)
                dk_s[at, :] = nt(qh, ds).astype(BF16)
                dq_s[at, :] = (nn(kt_s[row, at, :], ds) * 0.125).astype(BF16)
            at_turn(row * 6 + j, turns)
            return carry

        lax.fori_loop(0, 6, pair, 0)
        dx = []
        for g in range(4):
            lo = window(g)
            r = slice(192 * g, 192 * g + 192)
            cat = jnp.concatenate([dq_s[r, :], dk_s[r, :], dv_s[r, :]], axis=0)
            dx.append(nn(wt_ref[g], cat))
            gq = nn(cat, x_s[row, :, lo : lo + 256])
            keep = (lane < 192) if g % 2 == 0 else (lane >= 64)
            for c in range(3):
                gq_s[c, :, lo : lo + 256] += jnp.where(keep, gq[192 * c : 192 * c + 192], 0.0)
        gt_ref[row] = (res_s[row] + jnp.concatenate(dx, axis=0).T).astype(BF16)
        ones = jnp.ones((16, seq), BF16)
        gv2_s[0:1, :] += nt(ones, dq_s[...])[0:1]
        gv2_s[1:2, :] += nt(ones, dv_s[...])[0:1]
        return carry

    lax.fori_loop(0, n_rows, one_row, 0)
    slim, tall = gmq_ref.shape[1:]
    half = shares[3].half
    up = hot((192, tall), 0, n * tall)
    values = []
    for c in range(3):
        held = jnp.zeros((tall, 768), F32)
        for g in range(4):
            held = held + tn((0.95 * gmq_ref[4 * c + g]).astype(BF16), hot((slim, 768), 192 * g + d * slim, 0))
        values.append(gq_s[c] + nn(up, held.astype(BF16)))
    gv = jnp.concatenate([gv_ref[0:4], gv2_s[0:2], gv_ref[6:12]], axis=0)
    lane = lax.broadcasted_iota(jnp.int32, (192, 128), 1)
    for g in range(4):
        lo = window(g)
        tiles = []
        edges = []
        for c in range(3):
            a, b = values[c][:, lo : lo + 128], values[c][:, lo + 128 : lo + 256]
            whole, edge = (b, pltpu.roll(a, 64, 1)) if g % 2 else (a, b)
            tiles.append(whole)
            edges.append(jnp.where(lane < 64, edge, 0.0))
        tiles += [edges[0] + pltpu.roll(edges[1], 64, 1), edges[2]]
        vec = [gv[0:8, 192 * g : 192 * g + 128]]
        vec.append(jnp.concatenate([gv[0:8, 192 * g + 128 : 192 * g + 192], jnp.zeros((8, 64), F32)], axis=1))
        vec += [gv[8 + g : 9 + g, 128 * j : 128 * j + 128] for j in range(6)]
        vec.append(jnp.zeros((2 * half - 960 - 22, 128), F32))
        flat = jnp.concatenate(tiles + vec, axis=0).astype(BF16)
        sq_s[g * half : g * half + half, :] = flat[:half]
        sq_s[(4 + turned(g)) * half : (5 + turned(g)) * half, :] = flat[half:]
    for step in (q[0], f1[6], f2[6], q[1]):
        step()
    before = [[], [q[2]], [q[3]], [], []]
    between = [[], [], [], [q[4]], [q[5]]]

    def blocks(a_ref, b_ref):
        return jnp.concatenate([r[192 * j : 192 * j + 192, :] for r in (a_ref, b_ref) for j in range(3)], axis=1)

    def sweep(t, carry):
        @pl.when(jnp.logical_and(core0, t == 0))
        def _():
            yo_s[...] = ns_start([wide_rows(oo_s, 0, 4).astype(F32)])[0]

        @pl.when(jnp.logical_and(core1, t == 0))
        def _():
            for i, y in enumerate(ns_start([blocks(a, b).astype(F32) for a, b in ((f1_other, f1_half), (f2_other, f2_half))])):
                yf_s[i] = y

        @pl.when(core0)
        def _():
            mids, polys = ns_poly([yo_s[...]])
            mid_s[0:1, :] = jnp.broadcast_to(mids[0], (1, 128))
            po_s[...] = polys[0]

        @pl.when(core1)
        def _():
            mids, polys = ns_poly([yf_s[i] for i in range(2)])
            for i in range(2):
                mid_s[i : i + 1, :] = jnp.broadcast_to(mids[i], (1, 128))
                pf_s[i] = polys[i]

        at_turn(t, before)

        @pl.when(core0)
        def _():
            yo_s[...] = ns_step([yo_s[...]], [mid_s[0:1, 0:1]], [po_s[...]])[0]

        @pl.when(core1)
        def _():
            for i, y in enumerate(ns_step([yf_s[i] for i in range(2)], [mid_s[i : i + 1, 0:1] for i in range(2)], [pf_s[i] for i in range(2)])):
                yf_s[i] = y

        at_turn(t, between)
        return carry

    lax.fori_loop(0, NS_STEPS, sweep, 0)
    q[6]()
    wires = Wires(p, x_send, x_recv)
    me = 2 * p.x + p.y
    odd = lax.rem(me, 2) == 1
    around = ((1, 0), (0, 1), (1, 1))

    def scatter(src, dst):
        return [
            wires.plan_to(
                lambda dx=dx, dy=dy: src.at[lax.rem(p.x + dx, 2), lax.rem(p.y + dy, 2)], lambda: dst.at[me], lambda dx=dx, dy=dy: p.other(dx, dy)
            )
            for dx, dy in around
        ]

    early = [scatter(a, b) for a, b in ((tmf_s, rmf_s), (txf_s, rxf_s), (tmq_s, rmq_s), (tv_s, rv_s))]
    late = scatter(txq_s, rxq_s)
    sibling = lambda: p.device("c", 1)
    pass_early = [wires.plan_to(lambda a=a: a, lambda a=a: a, sibling) for a in (rmf_s, rxf_s, rmq_s, rv_s)]
    pass_late = [wires.plan_to(lambda: rxq_s, lambda: rxq_s, sibling)]
    pass_o = [wires.plan_to(lambda: xo_s, lambda: xo_r, sibling)]
    big = wo_ref.shape[2]
    sel_b = hot((big, 768), d * big, 0)
    wide, cols = w1_ref.shape[2], w1_ref.shape[1]

    def put_f(dst, pair):
        for x in range(2):
            sel = hot((cols, 192), (p.z * 2 + x) * cols, 0)
            part = jnp.concatenate([nn(sel, m) for m in pair], axis=0).astype(BF16)
            for y in range(2):
                dst[x, y] = part[:, 384 * y : 384 * y + 384]

    def put_q(dst, three):
        for x in range(2):
            part = jnp.zeros((192, 128), F32)
            for c, m in enumerate(three):
                at, s = canon(odd, (p.z * 2 + x) * slim)
                sel = jnp.logical_and(jnp.logical_and(at >= 0, at < slim), at + c * slim == s).astype(BF16)
                part = part + nn(m, sel)
            for y in range(2):
                dst[x, y] = part[96 * y : 96 * y + 96].astype(BF16)

    @pl.when(core0)
    def _():
        xo_s[...] = nn(sel_b, yo_s[...].astype(BF16)).astype(BF16)
        wires.start(pass_o)

    @pl.when(core1)
    def _():
        put_f(tmf_s, [blocks(f1_other, f1_half), blocks(f2_other, f2_half)])
        put_f(txf_s, [yf_s[i].astype(BF16) for i in range(2)])
        group = jnp.concatenate([q_other[...], q_half[...]], axis=0)
        tiles = [group[192 * j : 192 * j + 192] for j in range(5)]
        lane = lax.broadcasted_iota(jnp.int32, (192, 128), 1)
        pair = tiles[3].astype(F32)
        edges = [jnp.where(lane < 64, e, 0.0) for e in (pair, pltpu.roll(pair, 64, 1), tiles[4].astype(F32))]
        three = [jnp.concatenate([t.astype(F32), e], axis=1) for t, e in zip(tiles, edges)]
        put_q(tmq_s, [m.astype(BF16) for m in three])
        for x in range(2):
            for y in range(2):
                tv_s[x, y] = group[960:992]
        for copies in early:
            wires.start(copies)
        for a, b in ((tmf_s, rmf_s), (txf_s, rxf_s), (tmq_s, rmq_s), (tv_s, rv_s)):
            b[me] = a[p.x, p.y]
        for i, y in enumerate(ns_start(three)):
            yq_s[i] = y

        def turn(t, carry):
            ys = [yq_s[i] for i in range(3)]
            for i, y in enumerate(ns_step(ys, *ns_poly(ys))):
                yq_s[i] = y
            return carry

        lax.fori_loop(0, NS_STEPS, turn, 0)
        put_q(txq_s, [yq_s[i].astype(BF16) for i in range(3)])
        wires.start(late)
        rxq_s[me] = txq_s[p.x, p.y]
        for copies in early:
            wires.arrive(copies)
        wires.start(pass_early)
        wires.arrive(pass_o)

    @pl.when(core0)
    def _():
        wires.arrive(pass_early)

    def fresh(w, own, longest):
        return w - muon_rate * (0.2 * math.sqrt(longest) * own + muon_decay * w)

    sel_l = hot((wide, 768), n * wide, 0)
    sel_h = hot((wide, 384), p.c * wide, 0)
    sel_q = hot((tall, 96), p.c * tall, 0)
    mo_ref[0] = nt(sel_l, nn(sel_b, wide_rows(oo_s, 0, 4)).astype(BF16))
    no_ref[0] = fresh(wo_ref[0], nt(sel_l, jnp.where(core0, xo_s[...], xo_r[...])), 768)
    for g in range(4):
        for i, (w_ref, m_ref, n_ref) in enumerate(((w1_ref, m1_ref, n1_ref), (w2_ref, m2_ref, n2_ref))):
            at = slice(cols * i, cols * i + cols)
            m_ref[g] = nt(rmf_s[g, at, :], sel_h)
            n_ref[g] = fresh(w_ref[g], nt(rxf_s[g, at, :], sel_h), 768)
        own = nn(sel_q, rmq_s[g]).astype(BF16)
        for c in range(3):
            mq_ref[4 * c + g] = nt(hot((slim, 128), c * slim, 0), own)
    parts = [rv_s[g].astype(F32) for g in range(4)]
    top = jnp.concatenate([t for v in parts for t in (v[0:8], v[8:16, :64])], axis=1)
    low = [jnp.concatenate([v[16 + j : 17 + j] for j in range(6)], axis=1) for v in parts]
    grad = jnp.concatenate([top] + low, axis=0)
    first = 0.9 * vm1_ref[...] + 0.1 * grad
    second = 0.999 * vm2_ref[...] + 0.001 * grad * grad
    f_ref[...] = first
    s_ref[...] = second
    v_ref[...] = vec_ref[...] - adam_rate * (first * (1.0 / (1.0 - 0.9**STEP))) / (jnp.sqrt(second * (1.0 / (1.0 - 0.999**STEP))) + 1e-08)

    @pl.when(core1)
    def _():
        wires.arrive(late)
        wires.start(pass_late)

    @pl.when(core0)
    def _():
        wires.arrive(pass_late)

    for g in range(4):
        own = nn(sel_q, rxq_s[g]).astype(BF16)
        for c in range(3):
            nq_ref[4 * c + g] = fresh(wq_ref[4 * c + g], nt(hot((slim, 128), c * slim, 0), own), 192)

    @pl.when(core0)
    def _():
        wires.leave(pass_o)

    @pl.when(core1)
    def _():
        for copies in early + [late, pass_early, pass_late]:
            wires.leave(copies)


def closing_owned(p, shares, lengths, wt, so, s1, s2, gv, mq, weights, vec, vm1, vm2, acts, ident):
    tokens = acts[0]
    n, seq, d = tokens.shape
    slim = mq.shape[1]
    shape = lambda a: jax.ShapeDtypeStruct(a.shape, F32)
    outs = [jax.ShapeDtypeStruct(tokens.shape, BF16)] + [shape(w) for w in weights] * 2 + [shape(vec)] * 3
    hbm = pl.BlockSpec(memory_space=pl.ANY)
    tm, mt = pltpu.VMEM((n, seq, d), BF16), pltpu.VMEM((n, d, seq), BF16)
    scratch = [tm, mt, tm, mt, tm, mt, mt, pltpu.VMEM((n, seq, d), F32), pltpu.VMEM((seq, seq), F32)]
    scratch += [pltpu.VMEM((d, seq), BF16)] * 3 + [pltpu.VMEM((3, 192, 768), F32), pltpu.VMEM((8, 768), F32)]
    scratch += [pltpu.VMEM((shares[3].rows, 128), BF16), pltpu.VMEM((shares[0].rows, 128), BF16)]
    scratch += [pltpu.VMEM((768, 768), F32), pltpu.VMEM((768, 768), BF16), pltpu.VMEM((2, 192, 768), F32), pltpu.VMEM((3, 192, 256), F32)]
    scratch += [pltpu.VMEM((8, 128), F32), pltpu.VMEM((2, 192, 192), BF16)]
    scratch += [pltpu.VMEM((4 * slim, 768), BF16)] * 2
    to_f, to_q, to_v = (2 * slim, 384), (96, 128), (32, 128)
    scratch += [pltpu.VMEM((2, 2) + k, BF16) for k in (to_f, to_f, to_q, to_q, to_v)]
    scratch += [pltpu.VMEM((4,) + k, BF16) for k in (to_f, to_f, to_q, to_q, to_v)]
    scratch += [pltpu.SemaphoreType.DMA((n, 8)), pltpu.SemaphoreType.DMA((21,)), pltpu.SemaphoreType.DMA((21,))]
    scratch += shares[0].scratch(p)
    for s in shares[1:]:
        scratch += s.scratch()
    return pl.pallas_call(
        functools.partial(owner_kernel, p, shares),
        out_shape=outs,
        in_specs=[pl.BlockSpec(memory_space=pltpu.SMEM)] + [VMEM] * 13 + [hbm] * 6 + [VMEM] + [hbm] * 2,
        out_specs=[VMEM] * 12,
        scratch_shapes=scratch,
        compiler_params=pltpu.CompilerParams(collective_id=ident, has_side_effects=True, vmem_limit_bytes=62 * 2**20),
    )(lengths, wt, so, s1, s2, gv, mq, *weights, vec, vm1, vm2, *acts)


def hand_over_kernel(*refs):
    half = len(refs) // 2
    for src, dst in zip(refs[:half], refs[half:]):
        dst[...] = src[...]


def hand_over(values):
    return pl.pallas_call(
        hand_over_kernel,
        out_shape=[jax.ShapeDtypeStruct(a.shape, a.dtype) for a in values],
        in_specs=[VMEM] * len(values),
        out_specs=[VMEM] * len(values),
        compiler_params=pltpu.CompilerParams(vmem_limit_bytes=60 * 2**20),
    )(*values)


def local(tokens, doc_lengths, cotangent, qkv_weight, out_weight, ffn_in_weight, ffn_out_weight, vectors,
          qkv_moment, out_moment, ffn_in_moment, ffn_out_moment, vec_moment1, vec_moment2):
    p = Place(lax.axis_size("dp"), lax.axis_size("narrow"))
    flip = lambda a: a.transpose(0, 2, 1)
    wq, w1, w2, mq, m1, m2 = map(flip, (qkv_weight, ffn_in_weight, ffn_out_weight, qkv_moment, ffn_in_moment, ffn_out_moment))
    owned = p.X == 2 and p.Y == 2 and p.C == 2 and p.Z in (2, 4)
    if owned:
        shares = [Shares(p, 4608), Owned(p, 576), Owned(p, 576), Owned(p, 512)]
    else:
        shares = [Shares(p, r) for r in (4608, 4608, 4608, 3456 + 72)]
    qt, k, kt, v, ct, lse, w1p, w2p, wot, wt = opening(p, doc_lengths, tokens, wq, out_weight, w1, w2, vectors, 0)
    out_act, res, dct, so, s1, s2, gv = ffn(tokens, cotangent, ct, w1p, w2p, wot, vectors, out_moment, m1, m2, shares[0].rows, owned)
    acts = (tokens, qt, k, kt, v, ct, lse, dct, res)
    gt, gq, go, g1, g2, nq, no, n1, n2, f, s, vn = hand_over((closing_owned if owned else closing)(
        p, shares, doc_lengths, wt, so, s1, s2, gv, mq, (wq, out_weight, w1, w2), vectors, vec_moment1, vec_moment2, acts, 1))
    return (out_act, gt, flip(gq), go, flip(g1), flip(g2), flip(nq), no, flip(n1), flip(n2), f, s, vn)


def solution(mesh):
    rows = P(("dp", "narrow"), None, None)
    cut = P(None, "narrow", "dp")
    return jax.shard_map(
        local,
        mesh=mesh,
        in_specs=(rows, P(("dp", "narrow"), None), rows) + (cut,) * 4 + (P(),) + (cut,) * 4 + (P(), P()),
        out_specs=(rows, rows) + (cut,) * 8 + (P(),) * 3,
        check_vma=False,
    )
```

profile of v0, /device:TPU:0, one launch (start us, length us, event | category | flops | bytes accessed | tf_op | source)
XLA Modules:
  0.0 171.6 jit_solution(11981921552242696516)
XLA Ops:
  0.6 52.5 %shard_map.237 = (bf16[2,768,512]{2,1,0:T(8,128)(2,1)}, bf16[2,512,768]{2,1,0:T(8,128)(2,1)}, bf16[2,768,512]{2,1,0:T(8,128)(2,1)}, bf16[2,512,768]{2,1,0:T(8,12...) custom-call(s32[2,4]{1,0:T(2,128)} %refs_0_.1, ...), custom_call_target="tpu_custom_call" | custom-call | tf_op jit(solution)/shard_map/pallas_call | solution.py:637
  53.2 37.3 %shard_map.238 = (bf16[2,512,768]{2,1,0:T(8,128)(2,1)}, f32[2,512,768]{2,1,0:T(8,128)}, bf16[2,768,512]{2,1,0:T(8,128)(2,1)}, bf16[4608,128]{1,0:T(8,128)(2,1)},...) custom-call(bf16[2,512,768]{2,1,0:T(8,128)(2,1)} %refs_14_.1, ...), custom_call_target="tpu_custom_call" | custom-call | tf_op jit(solution)/shard_map/pallas_call | solution.py:201
  90.5 77.7 %shard_map.239 = (bf16[2,512,768]{2,1,0:T(8,128)(2,1)}, f32[12,24,48]{2,1,0:T(8,128)}, f32[1,192,96]{2,1,0:T(8,128)}, f32[4,24,192]{2,1,0:T(8,128)}, f32[4,24,19...) custom-call(s32[2,4]{1,0:T(2,128)} %refs_0_.1, ...), custom_call_target="tpu_custom_call" | custom-call | tf_op jit(solution)/shard_map/pallas_call | solution.py:1322
  168.2 3.2 %shard_map.240 = (bf16[2,512,768]{2,1,0:T(8,128)(2,1)}, f32[12,24,48]{2,1,0:T(8,128)}, f32[1,192,96]{2,1,0:T(8,128)}, f32[4,24,192]{2,1,0:T(8,128)}, f32[4,24,19...) custom-call(bf16[2,512,768]{2,1,0:T(8,128)(2,1)} %get-tuple-element., ...), custom_call_target="tpu_custom_call" | custom-call | tf_op jit(solution)/shard_map/pallas_call | solution.py:1339
where the time goes:
time: 172 us
  Pallas kernels  171 us (99%)
    pallas_call x1, Pallas kernels, closing_owned(): pl.pallas_call(functools.partial(owner_kernel, p, shares), out_shape=outs...  77.7 us
    pallas_call x1, Pallas kernels, opening(): pl.pallas_call(functools.partial(open_kernel, p), out_shape=[act(d, seq),...  52.5 us
    pallas_call x1, Pallas kernels, ffn(): pl.pallas_call(functools.partial(ffn_kernel, owned), grid=(n,), out_shape...  37.3 us

commit v1 on v0

--- a/solution.py
+++ b/solution.py
@@ -12,6 +12,7 @@
 MESH = pl.DeviceIdType.MESH
 NORM_EPS = 1e-05
 NS_STEPS = 5
+R_FIRST = 2
 STEP = 5
 ns_first = 3.4445
 ns_second = -4.775
@@ -76,15 +77,11 @@
 
 
 def gelu_parts(v):
-    u = jnp.abs(v) * 0.7071067811865476
-    den = 1.0 + 0.3275911 * u
-    t = pl.reciprocal(den, approx=True)
-    t = t * (2.0 - den * t)
-    ex = jnp.exp(-u * u)
-    poly = t * (0.254829592 + t * (-0.284496736 + t * (1.421413741 + t * (-1.453152027 + t * 1.061405429))))
-    half = 0.5 * poly * ex
+    t = pl.reciprocal(1.0 + (0.3275911 * 0.7071067811865476) * jnp.abs(v), approx=True)
+    ex = jnp.exp2(v * v * (-0.5 * 1.4426950408889634))
+    half = t * ex * (0.127414796 + t * (-0.142248368 + t * (0.7107068705 + t * (-0.7265760135 + t * 0.5307027145))))
     cdf = jnp.where(v >= 0, 1.0 - half, half)
-    return v * cdf, cdf + v * ex * 0.3989422804014327
+    return v * cdf, cdf + (v * ex) * 0.3989422804014327
 
 
 def norm(h):
@@ -108,64 +105,59 @@
 
 
 def ffn_kernel(owned, x_ref, cot_ref, ct_ref, w1_ref, w2_ref, wo_ref, vec_ref, mo_ref, m1_ref, m2_ref,
-               out_ref, res_ref, dct_ref, so_ref, s1_ref, s2_ref, gv_ref,
-               fl_s, act_s, slope_s, db_s, g1_ref, g2_ref, go_ref):
+               out_ref, res_ref, dct_ref, so_ref, s1_ref, s2_ref, gv_ref, g1_ref, g2_ref, go_ref):
     step = pl.program_id(0)
     T = x_ref.shape[1]
     vec = lambda i: vec_ref[i : i + 1, :]
-    x = x_ref[0].astype(F32)
-    ctx = ct_ref[0].T
-    h1 = x + (nn(ctx, wo_ref[...]) + vec(6))
+
+    @pl.when(step == 0)
+    def _():
+        g1_ref[...] = jnp.zeros_like(g1_ref)
+        g2_ref[...] = jnp.zeros_like(g2_ref)
+        go_ref[...] = jnp.zeros_like(go_ref)
+        gv_ref[...] = jnp.zeros_like(gv_ref)
+
+    h1 = x_ref[0].astype(F32) + (nn(ct_ref[0].T, wo_ref[...]) + vec(6))
     n1, inv1 = norm(h1)
     first = n1 * vec(0) + vec(1)
-    fl_s[...] = first.astype(BF16)
-    branch = []
+    fl = first.astype(BF16)
+    inner = lambda g: nn(fl[:, window(g) : window(g) + 256], w1_ref[g]) + vec(8 + g)
+    active, slope, branch = [], [], []
+    ahead = inner(0)
     for g in range(4):
-        lo = window(g)
-        inner = nn(fl_s[:, lo : lo + 256], w1_ref[g]) + vec(8 + g)
-        a, sl = gelu_parts(inner)
-        act_s[g] = a.astype(BF16)
-        slope_s[g] = sl
-        branch.append(nt(act_s[g], w2_ref[g]))
+        now, ahead = ahead, (inner(g + 1) if g < 3 else None)
+        a, sl = gelu_parts(now)
+        active.append(a.astype(BF16))
+        slope.append(sl)
+        branch.append(nt(active[g], w2_ref[g]))
     h2 = first + (join(branch) + vec(7))
     n2, inv2 = norm(h2)
     out_ref[0] = (n2 * vec(2) + vec(3)).astype(BF16)
     dy = cot_ref[0].astype(F32)
     dh2 = norm_back(dy, n2, inv2, vec(2))
     dbl = dh2.astype(BF16)
-    db_s[...] = dbl
     dbt = dbl.T
-    flt = fl_s[...].T
+    flt = fl.T
     ones = jnp.ones((16, T), BF16)
     dfirst = []
     gb = []
-
-    @pl.when(step == 0)
-    def _():
-        g1_ref[...] = jnp.zeros_like(g1_ref)
-        g2_ref[...] = jnp.zeros_like(g2_ref)
-        go_ref[...] = jnp.zeros_like(go_ref)
-        gv_ref[...] = jnp.zeros_like(gv_ref)
-
     for g in range(4):
-        lo = window(g)
-        da = nn(db_s[:, lo : lo + 256], w2_ref[g])
-        di = (da * slope_s[g]).astype(BF16)
+        da = nn(dbl[:, window(g) : window(g) + 256], w2_ref[g])
+        di = (da * slope[g]).astype(BF16)
         dfirst.append(nt(di, w1_ref[g]))
-        g2_ref[g] += nn(dbt[192 * g : 192 * g + 192, :], act_s[g])
+        g2_ref[g] += nn(dbt[192 * g : 192 * g + 192, :], active[g])
         ext = nn(jnp.concatenate([flt[192 * g : 192 * g + 192, :], ones], axis=0), di)
         g1_ref[g] += ext[:192]
         gb.append(ext[192:193])
     df = dh2 + join(dfirst)
     dh1 = norm_back(df, n1, inv1, vec(0))
-    res_ref[0] = dh1
     dat = dh1.astype(BF16)
+    res_ref[0] = dat
     go_ref[...] += nn(ct_ref[0], dat)
     dct_ref[0] = nt(wo_ref[...], dat).astype(BF16)
-    z = jnp.zeros((1, x.shape[1]), F32)
+    z = jnp.zeros((1, dy.shape[1]), F32)
     gv_ref[...] += jnp.concatenate(
         [col_sum(df * n1), col_sum(df), col_sum(dy * n2), col_sum(dy), z, z, col_sum(dat.astype(F32)), col_sum(dbl.astype(F32))] + gb, axis=0)
-
 
     @pl.when(step == pl.num_programs(0) - 1)
     def _():
@@ -203,7 +195,7 @@
         grid=(n,),
         out_shape=[
             jax.ShapeDtypeStruct((n, seq, d), BF16),
-            jax.ShapeDtypeStruct((n, seq, d), F32),
+            jax.ShapeDtypeStruct((n, seq, d), BF16),
             jax.ShapeDtypeStruct((n, d, seq), BF16),
         ]
         + [jax.ShapeDtypeStruct((rows, 128), BF16)] * 3
@@ -211,7 +203,6 @@
         in_specs=[act, act, actt, full(4, 256, 768), full(4, 256, 768), full(768, 768), full(12, 768), full(*mo.shape), full(*m1.shape), full(*m2.shape)],
         out_specs=[act, act, actt] + [full(rows, 128)] * 3 + [full(12, 768)],
         scratch_shapes=[
-            pltpu.VMEM((T, d), BF16), pltpu.VMEM((4, T, 768), BF16), pltpu.VMEM((4, T, 768), F32), pltpu.VMEM((T, d), BF16),
             pltpu.VMEM((4, 192, 768), F32), pltpu.VMEM((4, 192, 768), F32), pltpu.VMEM((768, 768), F32),
         ],
         compiler_params=pltpu.CompilerParams(vmem_limit_bytes=60 * 2**20),
@@ -240,17 +231,26 @@
         where[axis] = self.at(axis, j)
         return (where["z"] * self.X + where["x"], where["y"] * self.C + where["c"])
 
-    def other(self, dx, dy):
-        return (self.z * self.X + lax.rem(self.x + dx, self.X), lax.rem(self.y + dy, self.Y) * self.C + self.c)
+    def other(self, dx, dy, c):
+        return (self.z * self.X + lax.rem(self.x + dx, self.X), lax.rem(self.y + dy, self.Y) * self.C + c)
 
     def barrier(self, corner=False):
+        self.greet(corner)
+        self.meet(corner)
+
+    def greet(self, corner=False):
         sem = pltpu.get_barrier_semaphore()
         if corner:
-            pl.semaphore_signal(sem, inc=1, device_id=self.other(1, 1), device_id_type=MESH)
+            for c in range(self.C):
+                pl.semaphore_signal(sem, inc=1, device_id=self.other(1, 1, c), device_id_type=MESH)
+            for dx, dy in ((1, 0), (0, 1)):
+                pl.semaphore_signal(sem, inc=1, device_id=self.other(dx, dy, 1 - self.c), device_id_type=MESH)
         for axis in "zxyc":
             for j in range(1, getattr(self, axis.upper())):
                 pl.semaphore_signal(sem, inc=1, device_id=self.device(axis, j), device_id_type=MESH)
-        pl.semaphore_wait(sem, self.count() + int(corner))
+
+    def meet(self, corner=False):
+        pl.semaphore_wait(pltpu.get_barrier_semaphore(), self.count() + 4 * int(corner))
 
 
 class Wires:
@@ -513,6 +513,7 @@
                 qt_out, k_out, kt_out, v_out, ct_out, lse_ref, w1_out, w2_out, wo_out, wt_out,
                 bufq, bufr, win_s, qt_s, k_s, kt_s, v_s, ct_s, vt_s, bias_s, vcol_s, send_q, recv_q, send_r, recv_r, out_sem):
     p.locate()
+    p.greet()
     n_rows, seq = x_ref.shape[:2]
     odd = lax.rem(lax.axis_index("narrow"), 2) == 1
     slim, tall = wq_ref.shape[1:]
@@ -532,13 +533,13 @@
     if bufr.shape[4] > 3 * size:
         folded = jnp.concatenate([folded, jnp.zeros((bufr.shape[4] - 3 * size, 128), F32)], axis=0)
     bufr[p.z, p.c, p.x, p.y] = folded.astype(BF16)
-    p.barrier()
+    p.meet()
     wires_q, wires_r = Wires(p, send_q, recv_q), Wires(p, send_r, recv_r)
     steps_q = gather_steps(p, wires_q, bufq, qrows // 32 * 16)
     steps_r = gather_steps(p, wires_r, bufr, bufr.shape[4] // 32 * 16)
     for i, step in enumerate(steps_q):
         step()
-        if i == 2:
+        if i == R_FIRST:
             steps_r[0]()
     total = jnp.zeros((3 * 192, 1024), F32)
     dp = p.Z * p.X
@@ -563,7 +564,7 @@
             win_s[c, g, off : off + 192, :] = stack[192 * c : 192 * c + 192]
         wt_out[g] = nt(hot((192, 256), off, 0), stack).astype(BF16)
     vcol_s[...] = vec_ref[0:8, :].T
-    turns = dealt(steps_r[1:], 6 * n_rows)
+    turns = dealt(steps_r[1:], 3 * n_rows)
 
     def out_copies(row, which=range(5)):
         pairs = ((qt_s, qt_out), (k_s, k_out), (kt_s, kt_out), (v_s, v_out), (ct_s, ct_out))
@@ -588,24 +589,27 @@
         for copy in out_copies(row, range(4)):
             copy.start()
 
-        def pair(j, carry):
-            lo = pl.multiple_of(128 * j, 128)
-            kp = k_s[row, :, pl.ds(lo, 128)]
-            for e in range(2):
-                at = pl.ds(pl.multiple_of(lo + 64 * e, 64), 64)
+        def four(j, carry):
+            heads = [(pl.multiple_of(256 * j + 128 * u, 128), e) for u in range(2) for e in range(2)]
+            spots = [pl.ds(pl.multiple_of(lo + 64 * e, 64), 64) for lo, e in heads]
+            scores = []
+            for (lo, e), at in zip(heads, spots):
                 qh = qt_s[row, at, :]
                 none = jnp.zeros_like(qh)
-                s = nn(kp, jnp.concatenate([none, qh] if e else [qh, none], axis=0)) + bias_s[...]
+                scores.append(nn(k_s[row, :, pl.ds(lo, 128)], jnp.concatenate([none, qh] if e else [qh, none], axis=0)))
+            soft = []
+            for s in scores:
+                s = s + bias_s[...]
                 m = jnp.max(s, axis=0, keepdims=True)
                 ex = jnp.exp(s - m)
-                tot = jnp.sum(ex, axis=0, keepdims=True)
-                ctx = nn(vt_s[at, :], ex.astype(BF16))
-                ct_s[row, at, :] = (ctx * (1.0 / tot)).astype(BF16)
-                lse_ref[row, pl.ds(2 * j + e, 1), :] = m + jnp.log(tot)
-            at_turn(row * 6 + j, turns)
+                soft.append((m, ex.astype(BF16), jnp.sum(ex, axis=0, keepdims=True)))
+            for i, (at, (m, ex, tot)) in enumerate(zip(spots, soft)):
+                ct_s[row, at, :] = (nn(vt_s[at, :], ex) * (1.0 / tot)).astype(BF16)
+                lse_ref[row, pl.ds(4 * j + i, 1), :] = m + jnp.log(tot)
+            at_turn(row * 3 + j, turns)
             return carry
 
-        lax.fori_loop(0, 6, pair, 0)
+        lax.fori_loop(0, 3, four, 0)
         out_copies(row, (4,))[0].start()
         return carry
 
@@ -912,7 +916,7 @@
     hbm = pl.BlockSpec(memory_space=pl.ANY)
     tm, mt = pltpu.VMEM((n, seq, d), BF16), pltpu.VMEM((n, d, seq), BF16)
     flat = lambda r: pltpu.VMEM((r, 128), BF16)
-    scratch = [tm, mt, tm, mt, tm, mt, mt, pltpu.VMEM((n, seq, d), F32), pltpu.VMEM((seq, seq), F32)]
+    scratch = [tm, mt, tm, mt, tm, mt, mt, pltpu.VMEM((n, seq, d), BF16), pltpu.VMEM((seq, seq), F32)]
     scratch += [pltpu.VMEM((d, seq), BF16)] * 3 + [pltpu.VMEM((3, 192, 768), F32), pltpu.VMEM((8, 768), F32)]
     scratch += [flat(shares[3].rows)] + [flat(s.rows) for s in shares]
     scratch += [pltpu.VMEM((1536, 768), F32), pltpu.VMEM((768, 768), BF16), pltpu.VMEM((8, 192, 192), BF16), pltpu.VMEM((8, 128), F32)]
@@ -1005,6 +1009,64 @@
     return [functools.partial(step, t) for t in range(7)]
 
 
+class Solo:
+    def __init__(self, p, half):
+        self.half, self.rows, self.copies = half, 8 * half, 1 + 4 + 4 * (p.Z - 1)
+        q = (p.Z - 1) * (half // p.Z)
+        self.kinds = [8 * half, 8 * half] + [2 * half, half, q] * 2 + [2 * half]
+
+    def scratch(self):
+        return [pltpu.VMEM((k, 128), BF16) for k in self.kinds] + [pltpu.SemaphoreType.DMA((self.copies,))] * 2
+
+
+def solo_steps(p, s, src, scratch):
+    held, from_c, a1, a2, a3, b1, b2, b3, mine, send_sem, recv_sem = scratch
+    wires = Wires(p, send_sem, recv_sem)
+    h, q, z = s.half, s.half // p.Z, p.z
+    cut = lambda ref, start, size: lambda: ref.at[spread(start(), size)]
+    over = [wires.plan_to(lambda: src, lambda: from_c, lambda: p.device("c", 1))]
+    sends = [[], [], [], []]
+    ways = (("x", "y", p.x, p.y, 0, a1, a2, a3, 0), ("y", "x", p.y, p.x, 4 * h, b1, b2, b3, h))
+    for one, two, first, second, base, r1, r2, r3, to in ways:
+        sends[0].append(wires.plan(cut(held, lambda f=first, b=base: b + (1 - f) * 2 * h, 2 * h), lambda r=r1: r, one, 1))
+        sends[1].append(wires.plan(cut(held, lambda f=first, e=second, b=base: b + (2 * f + 1 - e) * h, h), lambda r=r2: r, two, 1))
+        for j in range(1, p.Z):
+            part = lambda f=first, e=second, b=base, j=j: b + (2 * f + e) * h + p.at("z", j) * q
+            sends[2].append(wires.plan(cut(held, part, q), lambda r=r3, j=j: r.at[pl.ds((j - 1) * q, q)], "z", j))
+            sends[3].append(wires.plan(*(cut(mine, lambda t=to: t + z * q, q),) * 2, "z", j))
+
+    def add(dst, to, ref, start, size, parts):
+        value = ref[spread(start, size), :].astype(F32)
+        for part in parts:
+            value = value + part.astype(F32)
+        dst[spread(to, size), :] = value.astype(BF16)
+
+    def give():
+        wires.start(over)
+
+    def gave():
+        wires.leave(over)
+
+    def step(t):
+        wires.arrive(over if t == 0 else sends[t - 1])
+        if t == 0:
+            held[...] = (src[...].astype(F32) + from_c[...].astype(F32)).astype(BF16)
+        for one, two, first, second, base, r1, r2, r3, to in ways:
+            spot = base + (2 * first + second) * h
+            if t == 1:
+                add(held, base + first * 2 * h, held, base + first * 2 * h, 2 * h, [r1[...]])
+            if t == 2:
+                add(held, spot, held, spot, h, [r2[...]])
+            if t == 3:
+                add(mine, to + z * q, held, spot + z * q, q, [r3[(j - 1) * q : j * q, :] for j in range(1, p.Z)])
+        if t < 4:
+            wires.start(sends[t])
+        else:
+            wires.finish(skip=over)
+
+    return give, gave, [functools.partial(step, t) for t in range(5)]
+
+
 def canon(odd, base):
     r = lax.broadcasted_iota(jnp.int32, (256, 128), 0)
     s = lax.broadcasted_iota(jnp.int32, (256, 128), 1)
@@ -1017,10 +1079,11 @@
      x_hbm, qt_hbm, k_hbm, kt_hbm, v_hbm, ct_hbm, lse_ref, dct_hbm, res_hbm,
      gt_ref, mq_ref, mo_ref, m1_ref, m2_ref, nq_ref, no_ref, n1_ref, n2_ref, f_ref, s_ref, v_ref,
      x_s, qt_s, k_s, kt_s, v_s, ct_s, dct_s, res_s, bias_s, dq_s, dk_s, dv_s, gq_s, gv2_s, sq_s, oo_s,
-     yo_s, po_s, yf_s, yq_s, mid_s, pf_s, xo_s, xo_r, tmf_s, txf_s, tmq_s, txq_s, tv_s, rmf_s, rxf_s, rmq_s, rxq_s, rv_s,
-     in_sem, x_send, x_recv) = refs[: 35 + 37]
-    rest = refs[35 + 37 :]
+     yo_s, yf_s, yq_s, xo_s, xo_r, tmf_s, txf_s, tmq_s, txq_s, tv_s, rmf_s, rxf_s, rmq_s, rxq_s, rv_s,
+     in_sem, x_send, x_recv) = refs[: 35 + 34]
+    rest = refs[35 + 34 :]
     p.locate()
+    p.greet(corner=True)
     d, n = lax.axis_index("dp"), lax.axis_index("narrow")
     core0, core1 = p.c == 0, p.c == 1
     n_rows, seq = x_s.shape[:2]
@@ -1032,15 +1095,18 @@
     for row in range(n_rows):
         for copy in loads(row):
             copy.start()
-    p.barrier(corner=True)
     o = sum_steps(p, shares[0], so_ref, oo_s, rest[:10])
     f1 = owned_steps(p, shares[1], s1_ref, rest[10:19])
     f2 = owned_steps(p, shares[2], s2_ref, rest[19:28])
-    q = owned_steps(p, shares[3], sq_s, rest[28:37])
-    f1_half, f1_other, f2_half, f2_other, q_half, q_other = rest[15], rest[16], rest[24], rest[25], rest[33], rest[34]
+    q_give, q_gave, q = solo_steps(p, shares[3], sq_s, rest[28:39])
+    q_all = rest[36]
+    f1_half, f1_other, f2_half, f2_other = rest[15], rest[16], rest[24], rest[25]
+    p.meet(corner=True)
     for step in (o[0], f1[0], f2[0]):
         step()
-    turns = dealt([o[1], f1[1], o[2], f2[1], o[3], f1[2], o[4], f2[2], f1[3], o[5], f2[3], o[6], f1[4], o[7], f2[4], f1[5], f2[5], o[8]], 6 * n_rows)
+    turns = [[] for _ in range(12 * n_rows)]
+    for i, step in ((0, f1[1]), (5, o[2]), (6, f2[1]), (9, f1[2]), (10, o[3]), (14, f2[2]), (14, f1[3]), (16, o[4]), (18, f2[3]), (22, f1[4]), (23, o[5])):
+        turns[i * n_rows // 2].append(step)
     gq_s[...] = jnp.zeros_like(gq_s)
     gv2_s[...] = jnp.zeros_like(gv2_s)
     lane = lax.broadcasted_iota(jnp.int32, (192, 256), 1)
@@ -1050,6 +1116,10 @@
         bias_s[...] = jnp.where(same, 0.0, -1e30)
         for copy in loads(row):
             copy.wait()
+
+        @pl.when(row == 0)
+        def _():
+            o[1]()
 
         def pair(j, carry):
             lo = pl.multiple_of(128 * j, 128)
@@ -1064,27 +1134,23 @@
                 ex = jnp.exp(s - lse_ref[row, pl.ds(2 * j + e, 1), :])
                 de = nn(vp, wide(dc))
                 ds = (ex * (de - delta)).astype(BF16)
-                dv_s[at, :] = nt(dc, ex.astype(BF16)).astype(BF16)
-                dk_s[at, :] = nt(qh, ds).astype(BF16)
-                dq_s[at, :] = (nn(kt_s[row, at, :], ds) * 0.125).astype(BF16)
-            at_turn(row * 6 + j, turns)
+                dv_s[row, at, :] = nt(dc, ex.astype(BF16)).astype(BF16)
+                dk_s[row, at, :] = nt(qh, ds).astype(BF16)
+                dq_s[row, at, :] = (nn(kt_s[row, at, :], ds) * 0.125).astype(BF16)
+                at_turn(row * 12 + 2 * j + e, turns)
             return carry
 
         lax.fori_loop(0, 6, pair, 0)
-        dx = []
         for g in range(4):
             lo = window(g)
             r = slice(192 * g, 192 * g + 192)
-            cat = jnp.concatenate([dq_s[r, :], dk_s[r, :], dv_s[r, :]], axis=0)
-            dx.append(nn(wt_ref[g], cat))
-            gq = nn(cat, x_s[row, :, lo : lo + 256])
+            gq = nn(jnp.concatenate([dq_s[row, r, :], dk_s[row, r, :], dv_s[row, r, :]], axis=0), x_s[row, :, lo : lo + 256])
             keep = (lane < 192) if g % 2 == 0 else (lane >= 64)
             for c in range(3):
                 gq_s[c, :, lo : lo + 256] += jnp.where(keep, gq[192 * c : 192 * c + 192], 0.0)
-        gt_ref[row] = (res_s[row] + jnp.concatenate(dx, axis=0).T).astype(BF16)
         ones = jnp.ones((16, seq), BF16)
-        gv2_s[0:1, :] += nt(ones, dq_s[...])[0:1]
-        gv2_s[1:2, :] += nt(ones, dv_s[...])[0:1]
+        gv2_s[0:1, :] += nt(ones, dq_s[row])[0:1]
+        gv2_s[1:2, :] += nt(ones, dv_s[row])[0:1]
         return carry
 
     lax.fori_loop(0, n_rows, one_row, 0)
@@ -1108,79 +1174,45 @@
             whole, edge = (b, pltpu.roll(a, 64, 1)) if g % 2 else (a, b)
             tiles.append(whole)
             edges.append(jnp.where(lane < 64, edge, 0.0))
-        tiles += [edges[0] + pltpu.roll(edges[1], 64, 1), edges[2]]
+        tiles.append(edges[0] + pltpu.roll(edges[1], 64, 1))
+        tiles.append(edges[2][:96] + pltpu.roll(edges[2][96:], 64, 1))
         vec = [gv[0:8, 192 * g : 192 * g + 128]]
         vec.append(jnp.concatenate([gv[0:8, 192 * g + 128 : 192 * g + 192], jnp.zeros((8, 64), F32)], axis=1))
         vec += [gv[8 + g : 9 + g, 128 * j : 128 * j + 128] for j in range(6)]
-        vec.append(jnp.zeros((2 * half - 960 - 22, 128), F32))
+        vec.append(jnp.zeros((2 * half - 864 - 22, 128), F32))
         flat = jnp.concatenate(tiles + vec, axis=0).astype(BF16)
         sq_s[g * half : g * half + half, :] = flat[:half]
         sq_s[(4 + turned(g)) * half : (5 + turned(g)) * half, :] = flat[half:]
-    for step in (q[0], f1[6], f2[6], q[1]):
-        step()
-    before = [[], [q[2]], [q[3]], [], []]
-    between = [[], [], [], [q[4]], [q[5]]]
-
     def blocks(a_ref, b_ref):
         return jnp.concatenate([r[192 * j : 192 * j + 192, :] for r in (a_ref, b_ref) for j in range(3)], axis=1)
 
-    def sweep(t, carry):
-        @pl.when(jnp.logical_and(core0, t == 0))
-        def _():
-            yo_s[...] = ns_start([wide_rows(oo_s, 0, 4).astype(F32)])[0]
-
-        @pl.when(jnp.logical_and(core1, t == 0))
-        def _():
-            for i, y in enumerate(ns_start([blocks(a, b).astype(F32) for a, b in ((f1_other, f1_half), (f2_other, f2_half))])):
-                yf_s[i] = y
-
-        @pl.when(core0)
-        def _():
-            mids, polys = ns_poly([yo_s[...]])
-            mid_s[0:1, :] = jnp.broadcast_to(mids[0], (1, 128))
-            po_s[...] = polys[0]
-
-        @pl.when(core1)
-        def _():
-            mids, polys = ns_poly([yf_s[i] for i in range(2)])
-            for i in range(2):
-                mid_s[i : i + 1, :] = jnp.broadcast_to(mids[i], (1, 128))
-                pf_s[i] = polys[i]
-
-        at_turn(t, before)
-
-        @pl.when(core0)
-        def _():
-            yo_s[...] = ns_step([yo_s[...]], [mid_s[0:1, 0:1]], [po_s[...]])[0]
-
-        @pl.when(core1)
-        def _():
-            for i, y in enumerate(ns_step([yf_s[i] for i in range(2)], [mid_s[i : i + 1, 0:1] for i in range(2)], [pf_s[i] for i in range(2)])):
-                yf_s[i] = y
-
-        at_turn(t, between)
-        return carry
-
-    lax.fori_loop(0, NS_STEPS, sweep, 0)
-    q[6]()
+    def grad_in(row):
+        dx = []
+        for g in range(4):
+            r = slice(192 * g, 192 * g + 192)
+            dx.append(nn(wt_ref[g], jnp.concatenate([dq_s[row, r, :], dk_s[row, r, :], dv_s[row, r, :]], axis=0)))
+        gt_ref[row] = (res_s[row].astype(F32) + jnp.concatenate(dx, axis=0).T).astype(BF16)
+
     wires = Wires(p, x_send, x_recv)
     me = 2 * p.x + p.y
     odd = lax.rem(me, 2) == 1
     around = ((1, 0), (0, 1), (1, 1))
 
-    def scatter(src, dst):
+    def scatter(src, dst, cores=(1,)):
         return [
             wires.plan_to(
-                lambda dx=dx, dy=dy: src.at[lax.rem(p.x + dx, 2), lax.rem(p.y + dy, 2)], lambda: dst.at[me], lambda dx=dx, dy=dy: p.other(dx, dy)
+                lambda dx=dx, dy=dy: src.at[lax.rem(p.x + dx, 2), lax.rem(p.y + dy, 2)], lambda: dst.at[me], lambda dx=dx, dy=dy, c=c: p.other(dx, dy, c)
             )
             for dx, dy in around
+            for c in cores
         ]
 
     early = [scatter(a, b) for a, b in ((tmf_s, rmf_s), (txf_s, rxf_s), (tmq_s, rmq_s), (tv_s, rv_s))]
-    late = scatter(txq_s, rxq_s)
+    late = scatter(txq_s, rxq_s, (0, 1))
+    late += [wires.plan_to(lambda: txq_s.at[p.x, p.y], lambda: rxq_s.at[me], lambda: p.device("c", 1))]
+    late_on = {0: [late[0], late[2], late[4], late[6]], 1: [late[1], late[3], late[5]]}
     sibling = lambda: p.device("c", 1)
     pass_early = [wires.plan_to(lambda a=a: a, lambda a=a: a, sibling) for a in (rmf_s, rxf_s, rmq_s, rv_s)]
-    pass_late = [wires.plan_to(lambda: rxq_s, lambda: rxq_s, sibling)]
     pass_o = [wires.plan_to(lambda: xo_s, lambda: xo_r, sibling)]
     big = wo_ref.shape[2]
     sel_b = hot((big, 768), d * big, 0)
@@ -1205,27 +1237,49 @@
 
     @pl.when(core0)
     def _():
+        q_give()
+        for step in (lambda: grad_in(0), o[6], f2[4], lambda: grad_in(1), f1[5], f2[5], o[7], o[8], f1[6], f2[6]):
+            step()
+        yo_s[...] = ns_start([wide_rows(oo_s, 0, 4).astype(F32)])[0]
+
+        def turn(t, carry):
+            y = yo_s[...]
+            yo_s[...] = ns_step([y], *ns_poly([y]))[0]
+            return carry
+
+        lax.fori_loop(0, NS_STEPS, turn, 0)
         xo_s[...] = nn(sel_b, yo_s[...].astype(BF16)).astype(BF16)
         wires.start(pass_o)
+        q_gave()
 
     @pl.when(core1)
     def _():
+        for step in (q[0], o[6], f2[4], lambda: grad_in(0), q[1], lambda: grad_in(1), f1[5], f2[5], o[7], o[8], q[2], f1[6], f2[6]):
+            step()
+        for i, y in enumerate(ns_start([blocks(a, b).astype(F32) for a, b in ((f1_other, f1_half), (f2_other, f2_half))])):
+            yf_s[i] = y
+
+        def f_turn(t, carry):
+            ys = [yf_s[i] for i in range(2)]
+            for i, y in enumerate(ns_step(ys, *ns_poly(ys))):
+                yf_s[i] = y
+            return carry
+
+        lax.fori_loop(0, 3, f_turn, 0)
+        q[3]()
+        lax.fori_loop(3, NS_STEPS, f_turn, 0)
         put_f(tmf_s, [blocks(f1_other, f1_half), blocks(f2_other, f2_half)])
         put_f(txf_s, [yf_s[i].astype(BF16) for i in range(2)])
-        group = jnp.concatenate([q_other[...], q_half[...]], axis=0)
-        tiles = [group[192 * j : 192 * j + 192] for j in range(5)]
+        for a, b, copies in zip((tmf_s, txf_s), (rmf_s, rxf_s), early[:2]):
+            wires.start(copies)
+            b[me] = a[p.x, p.y]
+        q[4]()
+        tiles = [q_all[192 * j : 192 * j + 192, :].astype(F32) for j in range(4)]
         lane = lax.broadcasted_iota(jnp.int32, (192, 128), 1)
-        pair = tiles[3].astype(F32)
-        edges = [jnp.where(lane < 64, e, 0.0) for e in (pair, pltpu.roll(pair, 64, 1), tiles[4].astype(F32))]
-        three = [jnp.concatenate([t.astype(F32), e], axis=1) for t, e in zip(tiles, edges)]
-        put_q(tmq_s, [m.astype(BF16) for m in three])
-        for x in range(2):
-            for y in range(2):
-                tv_s[x, y] = group[960:992]
-        for copies in early:
-            wires.start(copies)
-        for a, b in ((tmf_s, rmf_s), (txf_s, rxf_s), (tmq_s, rmq_s), (tv_s, rv_s)):
-            b[me] = a[p.x, p.y]
+        last = q_all[768:864, :].astype(F32)
+        last = jnp.concatenate([last, pltpu.roll(last, 64, 1)], axis=0)
+        edges = [jnp.where(lane < 64, e, 0.0) for e in (tiles[3], pltpu.roll(tiles[3], 64, 1), last)]
+        three = [jnp.concatenate([t, e], axis=1) for t, e in zip(tiles, edges)]
         for i, y in enumerate(ns_start(three)):
             yq_s[i] = y
 
@@ -1239,14 +1293,21 @@
         put_q(txq_s, [yq_s[i].astype(BF16) for i in range(3)])
         wires.start(late)
         rxq_s[me] = txq_s[p.x, p.y]
-        for copies in early:
+        put_q(tmq_s, [m.astype(BF16) for m in three])
+        for x in range(2):
+            for y in range(2):
+                tv_s[x, y] = q_all[864:896, :]
+        for a, b, copies in zip((tmq_s, tv_s), (rmq_s, rv_s), early[2:]):
+            wires.start(copies)
+            b[me] = a[p.x, p.y]
+        for copies in early[:2]:
             wires.arrive(copies)
-        wires.start(pass_early)
+        wires.start(pass_early[:2])
         wires.arrive(pass_o)
 
     @pl.when(core0)
     def _():
-        wires.arrive(pass_early)
+        wires.arrive(pass_early[:2])
 
     def fresh(w, own, longest):
         return w - muon_rate * (0.2 * math.sqrt(longest) * own + muon_decay * w)
@@ -1261,6 +1322,28 @@
             at = slice(cols * i, cols * i + cols)
             m_ref[g] = nt(rmf_s[g, at, :], sel_h)
             n_ref[g] = fresh(w_ref[g], nt(rxf_s[g, at, :], sel_h), 768)
+
+    @pl.when(core1)
+    def _():
+        for copies in early[2:]:
+            wires.arrive(copies)
+        wires.start(pass_early[2:])
+        wires.arrive(late_on[1])
+
+    @pl.when(core0)
+    def _():
+        wires.arrive(late_on[0])
+
+    for g in range(4):
+        own = nn(sel_q, rxq_s[g]).astype(BF16)
+        for c in range(3):
+            nq_ref[4 * c + g] = fresh(wq_ref[4 * c + g], nt(hot((slim, 128), c * slim, 0), own), 192)
+
+    @pl.when(core0)
+    def _():
+        wires.arrive(pass_early[2:])
+
+    for g in range(4):
         own = nn(sel_q, rmq_s[g]).astype(BF16)
         for c in range(3):
             mq_ref[4 * c + g] = nt(hot((slim, 128), c * slim, 0), own)
@@ -1274,27 +1357,13 @@
     s_ref[...] = second
     v_ref[...] = vec_ref[...] - adam_rate * (first * (1.0 / (1.0 - 0.9**STEP))) / (jnp.sqrt(second * (1.0 / (1.0 - 0.999**STEP))) + 1e-08)
 
-    @pl.when(core1)
-    def _():
-        wires.arrive(late)
-        wires.start(pass_late)
-
-    @pl.when(core0)
-    def _():
-        wires.arrive(pass_late)
-
-    for g in range(4):
-        own = nn(sel_q, rxq_s[g]).astype(BF16)
-        for c in range(3):
-            nq_ref[4 * c + g] = fresh(wq_ref[4 * c + g], nt(hot((slim, 128), c * slim, 0), own), 192)
-
     @pl.when(core0)
     def _():
         wires.leave(pass_o)
 
     @pl.when(core1)
     def _():
-        for copies in early + [late, pass_early, pass_late]:
+        for copies in early + [late, pass_early]:
             wires.leave(copies)
 
 
@@ -1306,16 +1375,15 @@
     outs = [jax.ShapeDtypeStruct(tokens.shape, BF16)] + [shape(w) for w in weights] * 2 + [shape(vec)] * 3
     hbm = pl.BlockSpec(memory_space=pl.ANY)
     tm, mt = pltpu.VMEM((n, seq, d), BF16), pltpu.VMEM((n, d, seq), BF16)
-    scratch = [tm, mt, tm, mt, tm, mt, mt, pltpu.VMEM((n, seq, d), F32), pltpu.VMEM((seq, seq), F32)]
-    scratch += [pltpu.VMEM((d, seq), BF16)] * 3 + [pltpu.VMEM((3, 192, 768), F32), pltpu.VMEM((8, 768), F32)]
+    scratch = [tm, mt, tm, mt, tm, mt, mt, pltpu.VMEM((n, seq, d), BF16), pltpu.VMEM((seq, seq), F32)]
+    scratch += [mt] * 3 + [pltpu.VMEM((3, 192, 768), F32), pltpu.VMEM((8, 768), F32)]
     scratch += [pltpu.VMEM((shares[3].rows, 128), BF16), pltpu.VMEM((shares[0].rows, 128), BF16)]
-    scratch += [pltpu.VMEM((768, 768), F32), pltpu.VMEM((768, 768), BF16), pltpu.VMEM((2, 192, 768), F32), pltpu.VMEM((3, 192, 256), F32)]
-    scratch += [pltpu.VMEM((8, 128), F32), pltpu.VMEM((2, 192, 192), BF16)]
+    scratch += [pltpu.VMEM((768, 768), F32), pltpu.VMEM((2, 192, 768), F32), pltpu.VMEM((3, 192, 256), F32)]
     scratch += [pltpu.VMEM((4 * slim, 768), BF16)] * 2
     to_f, to_q, to_v = (2 * slim, 384), (96, 128), (32, 128)
     scratch += [pltpu.VMEM((2, 2) + k, BF16) for k in (to_f, to_f, to_q, to_q, to_v)]
     scratch += [pltpu.VMEM((4,) + k, BF16) for k in (to_f, to_f, to_q, to_q, to_v)]
-    scratch += [pltpu.SemaphoreType.DMA((n, 8)), pltpu.SemaphoreType.DMA((21,)), pltpu.SemaphoreType.DMA((21,))]
+    scratch += [pltpu.SemaphoreType.DMA((n, 8)), pltpu.SemaphoreType.DMA((24,)), pltpu.SemaphoreType.DMA((24,))]
     scratch += shares[0].scratch(p)
     for s in shares[1:]:
         scratch += s.scratch()
@@ -1352,7 +1420,7 @@
     wq, w1, w2, mq, m1, m2 = map(flip, (qkv_weight, ffn_in_weight, ffn_out_weight, qkv_moment, ffn_in_moment, ffn_out_moment))
     owned = p.X == 2 and p.Y == 2 and p.C == 2 and p.Z in (2, 4)
     if owned:
-        shares = [Shares(p, 4608), Owned(p, 576), Owned(p, 576), Owned(p, 512)]
+        shares = [Shares(p, 4608), Owned(p, 576), Owned(p, 576), Solo(p, 448)]
     else:
         shares = [Shares(p, r) for r in (4608, 4608, 4608, 3456 + 72)]
     qt, k, kt, v, ct, lse, w1p, w2p, wot, wt = opening(p, doc_lengths, tokens, wq, out_weight, w1, w2, vectors, 0)

time: 172 us -> 168 us (0.977)
  Pallas kernels: 171 us -> 168 us
    pallas_call x1, Pallas kernels: 37.3 us -> 45.2 us  [ffn(): pl.pallas_call(functools.partial(ffn_kernel, owned), grid=(n,), out_shape...]
    pallas_call x1, Pallas kernels: 77.7 us -> 70 us  [closing_owned(): pl.pallas_call(functools.partial(owner_kernel, p, shares), out_shape=outs...]
    pallas_call x1, Pallas kernels: 52.5 us -> 49.8 us  [opening(): pl.pallas_call(functools.partial(open_kernel, p), out_shape=[act(d, seq),...]
where the time goes in v1:
time: 168 us; the launch traced here: 169 us
  Pallas kernels  168 us (100%)
    pallas_call x1, Pallas kernels, closing_owned(): pl.pallas_call(functools.partial(owner_kernel, p, shares), out_shape=outs...  70 us
    pallas_call x1, Pallas kernels, opening(): pl.pallas_call(functools.partial(open_kernel, p), out_shape=[act(d, seq),...  49.8 us
    pallas_call x1, Pallas kernels, ffn(): pl.pallas_call(functools.partial(ffn_kernel, owned), grid=(n,), out_shape...  45.2 us

profile of v1, /device:TPU:0, one launch (start us, length us, event | category | flops | bytes accessed | tf_op | source)
XLA Modules:
  0.0 169.1 jit_solution(5148627029066709529)
XLA Ops:
  0.6 49.8 %shard_map.237 = (bf16[2,768,512]{2,1,0:T(8,128)(2,1)}, bf16[2,512,768]{2,1,0:T(8,128)(2,1)}, bf16[2,768,512]{2,1,0:T(8,128)(2,1)}, bf16[2,512,768]{2,1,0:T(8,12...) custom-call(s32[2,4]{1,0:T(2,128)} %refs_0_.1, ...), custom_call_target="tpu_custom_call" | custom-call | tf_op jit(solution)/shard_map/pallas_call | solution.py:641
  50.4 45.2 %shard_map.238 = (bf16[2,512,768]{2,1,0:T(8,128)(2,1)}, bf16[2,512,768]{2,1,0:T(8,128)(2,1)}, bf16[2,768,512]{2,1,0:T(8,128)(2,1)}, bf16[4608,128]{1,0:T(8,128)(...) custom-call(bf16[2,512,768]{2,1,0:T(8,128)(2,1)} %refs_14_.1, ...), custom_call_target="tpu_custom_call" | custom-call | tf_op jit(solution)/shard_map/pallas_call | solution.py:193
  95.7 70.0 %shard_map.239 = (bf16[2,512,768]{2,1,0:T(8,128)(2,1)}, f32[12,24,48]{2,1,0:T(8,128)}, f32[1,192,96]{2,1,0:T(8,128)}, f32[4,24,192]{2,1,0:T(8,128)}, f32[4,24,19...) custom-call(s32[2,4]{1,0:T(2,128)} %refs_0_.1, ...), custom_call_target="tpu_custom_call" | custom-call | tf_op jit(solution)/shard_map/pallas_call | solution.py:1390
  165.7 3.2 %shard_map.240 = (bf16[2,512,768]{2,1,0:T(8,128)(2,1)}, f32[12,24,48]{2,1,0:T(8,128)}, f32[1,192,96]{2,1,0:T(8,128)}, f32[4,24,192]{2,1,0:T(8,128)}, f32[4,24,19...) custom-call(bf16[2,512,768]{2,1,0:T(8,128)(2,1)} %get-tuple-element., ...), custom_call_target="tpu_custom_call" | custom-call | tf_op jit(solution)/shard_map/pallas_call | solution.py:1407

commit v2 on v1

--- a/solution.py
+++ b/solution.py
@@ -12,7 +12,6 @@
 MESH = pl.DeviceIdType.MESH
 NORM_EPS = 1e-05
 NS_STEPS = 5
-R_FIRST = 2
 STEP = 5
 ns_first = 3.4445
 ns_second = -4.775
@@ -68,6 +67,16 @@
         dst[base + 192 * j : base + 192 * j + 192, :] = value[:, 128 * j : 128 * j + 128].astype(BF16)
 
 
+def add_blocks(dst, base, value):
+    for j in range(value.shape[1] // 128):
+        at = slice(base + 192 * j, base + 192 * j + 192)
+        dst[at, :] = (dst[at, :].astype(F32) + value[:, 128 * j : 128 * j + 128]).astype(BF16)
+
+
+def group_rows(owned, g):
+    return (576 * g, 2304 + 576 * turned(g)) if owned else (1152 * g, 1152 * g + 576)
+
+
 def wide_rows(ref, base, count):
     parts = []
     for q in range(count):
@@ -102,111 +111,6 @@
 
 def turned(g):
     return 2 * (g % 2) + g // 2
-
-
-def ffn_kernel(owned, x_ref, cot_ref, ct_ref, w1_ref, w2_ref, wo_ref, vec_ref, mo_ref, m1_ref, m2_ref,
-               out_ref, res_ref, dct_ref, so_ref, s1_ref, s2_ref, gv_ref, g1_ref, g2_ref, go_ref):
-    step = pl.program_id(0)
-    T = x_ref.shape[1]
-    vec = lambda i: vec_ref[i : i + 1, :]
-
-    @pl.when(step == 0)
-    def _():
-        g1_ref[...] = jnp.zeros_like(g1_ref)
-        g2_ref[...] = jnp.zeros_like(g2_ref)
-        go_ref[...] = jnp.zeros_like(go_ref)
-        gv_ref[...] = jnp.zeros_like(gv_ref)
-
-    h1 = x_ref[0].astype(F32) + (nn(ct_ref[0].T, wo_ref[...]) + vec(6))
-    n1, inv1 = norm(h1)
-    first = n1 * vec(0) + vec(1)
-    fl = first.astype(BF16)
-    inner = lambda g: nn(fl[:, window(g) : window(g) + 256], w1_ref[g]) + vec(8 + g)
-    active, slope, branch = [], [], []
-    ahead = inner(0)
-    for g in range(4):
-        now, ahead = ahead, (inner(g + 1) if g < 3 else None)
-        a, sl = gelu_parts(now)
-        active.append(a.astype(BF16))
-        slope.append(sl)
-        branch.append(nt(active[g], w2_ref[g]))
-    h2 = first + (join(branch) + vec(7))
-    n2, inv2 = norm(h2)
-    out_ref[0] = (n2 * vec(2) + vec(3)).astype(BF16)
-    dy = cot_ref[0].astype(F32)
-    dh2 = norm_back(dy, n2, inv2, vec(2))
-    dbl = dh2.astype(BF16)
-    dbt = dbl.T
-    flt = fl.T
-    ones = jnp.ones((16, T), BF16)
-    dfirst = []
-    gb = []
-    for g in range(4):
-        da = nn(dbl[:, window(g) : window(g) + 256], w2_ref[g])
-        di = (da * slope[g]).astype(BF16)
-        dfirst.append(nt(di, w1_ref[g]))
-        g2_ref[g] += nn(dbt[192 * g : 192 * g + 192, :], active[g])
-        ext = nn(jnp.concatenate([flt[192 * g : 192 * g + 192, :], ones], axis=0), di)
-        g1_ref[g] += ext[:192]
-        gb.append(ext[192:193])
-    df = dh2 + join(dfirst)
-    dh1 = norm_back(df, n1, inv1, vec(0))
-    dat = dh1.astype(BF16)
-    res_ref[0] = dat
-    go_ref[...] += nn(ct_ref[0], dat)
-    dct_ref[0] = nt(wo_ref[...], dat).astype(BF16)
-    z = jnp.zeros((1, dy.shape[1]), F32)
-    gv_ref[...] += jnp.concatenate(
-        [col_sum(df * n1), col_sum(df), col_sum(dy * n2), col_sum(dy), z, z, col_sum(dat.astype(F32)), col_sum(dbl.astype(F32))] + gb, axis=0)
-
-    @pl.when(step == pl.num_programs(0) - 1)
-    def _():
-        d, n = lax.axis_index("dp"), lax.axis_index("narrow")
-        slim, wide = m1_ref.shape[1:]
-        big = mo_ref.shape[2]
-        sel_l = hot((wide, 768), n * wide, 0)
-        sel_s = hot((192, slim), 0, d * slim)
-        placed = nt(hot((768, big), 0, d * big), (0.95 * mo_ref[0]).astype(BF16)).astype(BF16)
-        value = go_ref[...] + nn(placed, sel_l)
-        for q in range(4):
-            put_blocks(so_ref, 1152 * q, value[192 * q : 192 * q + 192])
-        for dst, g_ref, m_ref in ((s1_ref, g1_ref, m1_ref), (s2_ref, g2_ref, m2_ref)):
-            for g in range(4):
-                placed = nn(sel_s, (0.95 * m_ref[g]).astype(BF16)).astype(BF16)
-                value = g_ref[g] + nn(placed, sel_l)
-                if owned:
-                    put_blocks(dst, 576 * g, value[:, :384])
-                    put_blocks(dst, 2304 + 576 * turned(g), value[:, 384:])
-                else:
-                    put_blocks(dst, 1152 * g, value)
-        for dst in (so_ref, s1_ref, s2_ref):
-            if dst.shape[0] > 4608:
-                dst[4608:, :] = jnp.zeros((dst.shape[0] - 4608, 128), BF16)
-
-
-def ffn(tokens, cot, ct, w1, w2, wo, vec, mo, m1, m2, rows, owned):
-    n, seq, d = tokens.shape
-    T = seq
-    act = pl.BlockSpec((1, T, d), lambda i: (i, 0, 0))
-    actt = pl.BlockSpec((1, d, T), lambda i: (i, 0, 0))
-    full = lambda *s: pl.BlockSpec(s, lambda i: (0,) * len(s))
-    return pl.pallas_call(
-        functools.partial(ffn_kernel, owned),
-        grid=(n,),
-        out_shape=[
-            jax.ShapeDtypeStruct((n, seq, d), BF16),
-            jax.ShapeDtypeStruct((n, seq, d), BF16),
-            jax.ShapeDtypeStruct((n, d, seq), BF16),
-        ]
-        + [jax.ShapeDtypeStruct((rows, 128), BF16)] * 3
-        + [jax.ShapeDtypeStruct((12, 768), F32)],
-        in_specs=[act, act, actt, full(4, 256, 768), full(4, 256, 768), full(768, 768), full(12, 768), full(*mo.shape), full(*m1.shape), full(*m2.shape)],
-        out_specs=[act, act, actt] + [full(rows, 128)] * 3 + [full(12, 768)],
-        scratch_shapes=[
-            pltpu.VMEM((4, 192, 768), F32), pltpu.VMEM((4, 192, 768), F32), pltpu.VMEM((768, 768), F32),
-        ],
-        compiler_params=pltpu.CompilerParams(vmem_limit_bytes=60 * 2**20),
-    )(tokens, cot, ct, w1, w2, wo, vec, mo, m1, m2)
 
 
 class Place:
@@ -294,7 +198,7 @@
     return (p.Z - 1) + p.Z * ((p.X - 1) + (p.Y - 1) + 2 * (p.X - 1) * (p.Y - 1) + (p.C - 1))
 
 
-def gather_steps(p, wires, buf, half):
+def gather_steps(p, wires, buf, half, corner=False):
     z, x, y, c = p.z, p.x, p.y, p.c
     rest = buf.shape[4] - half
 
@@ -309,32 +213,35 @@
         mine = lambda f=from_z: (f(), c, x, y)
         first[i] = [wires.plan(*same(mine), "x", j) for j in range(1, p.X)] + [wires.plan(*same(mine), "y", j) for j in range(1, p.Y)]
         second[i] = []
-        for j in range(1, p.X):
+        if corner:
+            first[i].append(wires.plan_to(*same(mine), lambda: p.other(1, 1, c)))
+        for j in range(1, p.X if not corner else 1):
             part = lambda f=from_z, j=j: (f(), c, p.at("x", p.X - j), y, pl.ds(0, half))
             second[i] += [wires.plan(*same(part), "y", q) for q in range(1, p.Y)]
-        for j in range(1, p.Y):
+        for j in range(1, p.Y if not corner else 1):
             part = lambda f=from_z, j=j: (f(), c, x, p.at("y", p.Y - j), pl.ds(half, rest))
             second[i] += [wires.plan(*same(part), "x", q) for q in range(1, p.X)]
         last[i] = [wires.plan(*same(lambda f=from_z: (f(), c)), "c", j) for j in range(1, p.C)]
 
-    def step(t):
-        if t == 0:
-            wires.start(along.values())
-        if t < p.Z:
-            if t:
-                wires.arrive([along[t]])
-            wires.start(first[t])
-        if 1 <= t <= p.Z:
-            wires.arrive(first[t - 1])
-            wires.start(second[t - 1])
-        if 2 <= t <= p.Z + 1:
-            wires.arrive(second[t - 2])
-            wires.start(last[t - 2])
-        if t == p.Z + 2:
-            for i in last:
-                wires.arrive(last[i])
-
-    return [functools.partial(step, t) for t in range(p.Z + 3)]
+    def own(i):
+        if i:
+            wires.arrive([along[i]])
+        wires.start(first[i])
+
+    def onward(i):
+        wires.arrive(first[i])
+        wires.start(second[i])
+
+    def over(i):
+        wires.arrive(first[i] if corner else second[i])
+        wires.start(last[i])
+
+    def done():
+        for i in last:
+            wires.arrive(last[i])
+
+    of = lambda f: [functools.partial(f, i) for i in range(p.Z)]
+    return lambda: wires.start(along.values()), of(own), [] if corner else of(onward), of(over), done
 
 
 class Shares:
@@ -509,11 +416,12 @@
     return jnp.logical_and(rows + at == cols, rows < limit).astype(BF16)
 
 
-def open_kernel(p, len_ref, x_ref, wq_ref, wo_ref, w1_ref, w2_ref, vec_ref,
-                qt_out, k_out, kt_out, v_out, ct_out, lse_ref, w1_out, w2_out, wo_out, wt_out,
-                bufq, bufr, win_s, qt_s, k_s, kt_s, v_s, ct_s, vt_s, bias_s, vcol_s, send_q, recv_q, send_r, recv_r, out_sem):
+def front_kernel(p, owned, len_ref, x_ref, cot_ref, wq_ref, wo_ref, w1_ref, w2_ref, vec_ref, mo_ref, m1_ref, m2_ref,
+                 qt_out, k_out, kt_out, v_out, ct_out, out_out, res_out, dct_out, lse_ref, wt_out, so_ref, s1_ref, s2_ref, gv_ref,
+                 bufq, bufr, place_s, win_s, qt_s, k_s, kt_s, v_s, ct_s, vt_s, bias_s, vcol_s, w1_s, w2_s, wo_s, out_s, res_s, dct_s,
+                 send_q, recv_q, send_r, recv_r, out_sem):
     p.locate()
-    p.greet()
+    p.greet(corner=owned)
     n_rows, seq = x_ref.shape[:2]
     odd = lax.rem(lax.axis_index("narrow"), 2) == 1
     slim, tall = wq_ref.shape[1:]
@@ -524,6 +432,11 @@
         bufq[p.z, p.c, p.x, p.y, c * tall : c * tall + tall, :] = t.astype(BF16)
     if qrows > 3 * tall:
         bufq[p.z, p.c, p.x, p.y, 3 * tall :, :] = jnp.zeros((qrows - 3 * tall, 128), BF16)
+    p.meet(corner=owned)
+    wires_q, wires_r = Wires(p, send_q, recv_q), Wires(p, send_r, recv_r)
+    q_z, q_own, q_on, q_over, q_done = gather_steps(p, wires_q, bufq, qrows // 32 * 16, corner=owned)
+    q_z()
+    q_own[0]()
     rows, wide = 4 * slim, 4 * tall
     size = fold_rows(rows, wide)
     big = wo_ref.shape[2]
@@ -533,59 +446,91 @@
     if bufr.shape[4] > 3 * size:
         folded = jnp.concatenate([folded, jnp.zeros((bufr.shape[4] - 3 * size, 128), F32)], axis=0)
     bufr[p.z, p.c, p.x, p.y] = folded.astype(BF16)
-    p.meet()
-    wires_q, wires_r = Wires(p, send_q, recv_q), Wires(p, send_r, recv_r)
-    steps_q = gather_steps(p, wires_q, bufq, qrows // 32 * 16)
-    steps_r = gather_steps(p, wires_r, bufr, bufr.shape[4] // 32 * 16)
-    for i, step in enumerate(steps_q):
-        step()
-        if i == R_FIRST:
-            steps_r[0]()
+    d, n = lax.axis_index("dp"), lax.axis_index("narrow")
+    sel_l = hot((wide, 768), n * wide, 0)
+    placed = nt(hot((768, big), 0, d * big), (0.95 * mo_ref[0]).astype(BF16)).astype(BF16)
+    value = nn(placed, sel_l)
+    for q in range(4):
+        put_blocks(so_ref, 1152 * q, value[192 * q : 192 * q + 192])
+    for dst, m_ref in ((s1_ref, m1_ref), (s2_ref, m2_ref)):
+        for g in range(4):
+            value = nn(nn(hot((192, slim), 0, d * slim), (0.95 * m_ref[g]).astype(BF16)).astype(BF16), sel_l)
+            for half, base in enumerate(group_rows(owned, g)):
+                put_blocks(dst, base, value[:, 384 * half : 384 * half + 384])
+    for dst in (so_ref, s1_ref, s2_ref):
+        if dst.shape[0] > 4608:
+            dst[4608:, :] = jnp.zeros((dst.shape[0] - 4608, 128), BF16)
+    gv_ref[...] = jnp.zeros_like(gv_ref)
+    dp = p.Z * p.X
+    for pair in range(dp // 2):
+        r = lax.broadcasted_iota(jnp.int32, (256, 1), 0)
+        q = jnp.where(r < 128, r, r - 128)
+        g = (q >= slim).astype(jnp.int32) + (q >= 2 * slim).astype(jnp.int32) + (q >= 3 * slim).astype(jnp.int32)
+        col = 256 * g + jnp.where(jnp.logical_or(g == 1, g == 3), 64, 0) + jnp.where(r < 128, 2 * pair * slim, (2 * pair + 1) * slim) + q - g * slim
+        col = jnp.where(q < 4 * slim, col, -1)
+        place_s[pair] = (lax.broadcasted_iota(jnp.int32, (256, 1024), 1) == col).astype(BF16)
+    win_s[...] = jnp.zeros_like(win_s)
+    vcol_s[...] = vec_ref[0:8, :].T
+    r_z, r_own, r_on, r_over, r_done = gather_steps(p, wires_r, bufr, bufr.shape[4] // 32 * 16)
+    for t in range(1, p.Z + 2):
+        for steps, at in ((q_own, t), (q_on, t - 1), (q_over, t - (1 if owned else 2))):
+            if 0 <= at < len(steps):
+                steps[at]()
+        if t == p.Z - 2:
+            r_z()
+    r_own[0]()
+    q_done()
     total = jnp.zeros((3 * 192, 1024), F32)
-    dp = p.Z * p.X
     for pair in range(dp // 2):
         tiles = []
         for d in (2 * pair, 2 * pair + 1):
             z, x = d // p.X, d % p.X
             got = [bufq[z, c, x, y].astype(F32) for y in range(p.Y) for c in range(p.C)]
             tiles.append(jnp.concatenate([b[c * tall : c * tall + tall] for c in range(3) for b in got], axis=0))
-        r = lax.broadcasted_iota(jnp.int32, (256, 1), 0)
-        q = jnp.where(r < 128, r, r - 128)
-        g = (q >= slim).astype(jnp.int32) + (q >= 2 * slim).astype(jnp.int32) + (q >= 3 * slim).astype(jnp.int32)
-        col = 256 * g + jnp.where(jnp.logical_or(g == 1, g == 3), 64, 0) + jnp.where(r < 128, 2 * pair * slim, (2 * pair + 1) * slim) + q - g * slim
-        col = jnp.where(q < 4 * slim, col, -1)
-        place = (lax.broadcasted_iota(jnp.int32, (256, 1024), 1) == col).astype(BF16)
-        total = total + nn(jnp.concatenate(tiles, axis=1).astype(BF16), place)
-    win_s[...] = jnp.zeros_like(win_s)
+        total = total + nn(jnp.concatenate(tiles, axis=1).astype(BF16), place_s[pair])
     for g in range(4):
         off = 64 * (g % 2)
         stack = total[:, 256 * g : 256 * g + 256].astype(BF16)
         for c in range(3):
             win_s[c, g, off : off + 192, :] = stack[192 * c : 192 * c + 192]
         wt_out[g] = nt(hot((192, 256), off, 0), stack).astype(BF16)
-    vcol_s[...] = vec_ref[0:8, :].T
-    turns = dealt(steps_r[1:], 3 * n_rows)
-
-    def out_copies(row, which=range(5)):
-        pairs = ((qt_s, qt_out), (k_s, k_out), (kt_s, kt_out), (v_s, v_out), (ct_s, ct_out))
-        return [pltpu.make_async_copy(pairs[i][0].at[row], pairs[i][1].at[row], out_sem.at[row, i]) for i in which]
+    turns = [[] for _ in range(3 * n_rows)]
+    for i, step in enumerate(r_on):
+        turns[min(i, 3, len(turns) - 1)].append(step)
+    for i, step in enumerate(r_over):
+        turns[min(min(i, 3) // 2 + 3, len(turns) - 1)].append(step)
+    turns[-1].append(r_done)
+
+    for step in r_own[1:]:
+        step()
+
+    def out_copies(row, which):
+        pairs = ((qt_s, qt_out), (k_s, k_out), (kt_s, kt_out), (v_s, v_out), (ct_s.at[row], ct_out), (out_s, out_out), (res_s, res_out), (dct_s, dct_out))
+        return [pltpu.make_async_copy(pairs[i][0], pairs[i][1].at[row], out_sem.at[i]) for i in which]
+
+    def reuse(row, which):
+        @pl.when(row > 0)
+        def _():
+            for copy in out_copies(row - 1, which):
+                copy.wait()
 
     def one_row(row, carry):
         same = ids(len_ref, row, (seq, seq), 0) == ids(len_ref, row, (seq, seq), 1)
         bias_s[...] = jnp.where(same, 0.0, -1e30)
+        reuse(row, range(5))
         for g in range(4):
             lo = window(g)
             xw = x_ref[row, :, lo : lo + 256]
             off = 64 * (g % 2)
             r = slice(192 * g, 192 * g + 192)
             q = nt(win_s[0, g, off : off + 192, :], xw) + vcol_s[r, 4:5]
-            qt_s[row, r, :] = q.astype(BF16) * BF16(0.125)
-            kt_s[row, r, :] = nt(win_s[1, g, off : off + 192, :], xw).astype(BF16)
+            qt_s[r, :] = q.astype(BF16) * BF16(0.125)
+            kt_s[r, :] = nt(win_s[1, g, off : off + 192, :], xw).astype(BF16)
             v = nt(win_s[2, g, off : off + 192, :], xw) + vcol_s[r, 5:6]
             vt_s[r, :] = v.astype(BF16)
         wide_of = lambda c: join([nt(x_ref[row, :, window(g) : window(g) + 256], win_s[c, g]) for g in range(4)])
-        k_s[row] = wide_of(1).astype(BF16)
-        v_s[row] = (wide_of(2) + vec_ref[5:6, :]).astype(BF16)
+        k_s[...] = wide_of(1).astype(BF16)
+        v_s[...] = (wide_of(2) + vec_ref[5:6, :]).astype(BF16)
         for copy in out_copies(row, range(4)):
             copy.start()
 
@@ -594,9 +539,9 @@
             spots = [pl.ds(pl.multiple_of(lo + 64 * e, 64), 64) for lo, e in heads]
             scores = []
             for (lo, e), at in zip(heads, spots):
-                qh = qt_s[row, at, :]
+                qh = qt_s[at, :]
                 none = jnp.zeros_like(qh)
-                scores.append(nn(k_s[row, :, pl.ds(lo, 128)], jnp.concatenate([none, qh] if e else [qh, none], axis=0)))
+                scores.append(nn(k_s[:, pl.ds(lo, 128)], jnp.concatenate([none, qh] if e else [qh, none], axis=0)))
             soft = []
             for s in scores:
                 s = s + bias_s[...]
@@ -617,46 +562,105 @@
     wires_q.finish()
     wires_r.finish()
     whole = unfold(p, bufr, 0, rows, wide)
-    wo_out[...] = jnp.concatenate(whole, axis=0).astype(BF16)
-    for i, dst in enumerate((w1_out, w2_out)):
+    wo_s[...] = jnp.concatenate(whole, axis=0).astype(BF16)
+    for i, dst in enumerate((w1_s, w2_s)):
         whole = unfold(p, bufr, (i + 1) * size, rows, wide)
-        dst[...] = jnp.zeros_like(dst)
         for g in range(4):
             off = 64 * (g % 2)
             dst[g, off : off + 192, :] = jnp.concatenate([b[g * slim : g * slim + slim] for b in whole], axis=0).astype(BF16)
-    for row in range(n_rows):
-        for copy in out_copies(row):
-            copy.wait()
-
-
-def opening(p, lengths, tokens, wq, wo, w1, w2, vec, ident):
+            dst[g, 192 - 192 * (g % 2) : 256 - 192 * (g % 2), :] = jnp.zeros((64, 768), BF16)
+    vec = lambda i: vec_ref[i : i + 1, :]
+
+    def feed_forward(row, carry):
+        h1 = x_ref[row].astype(F32) + (nn(ct_s[row].T, wo_s[...]) + vec(6))
+        n1, inv1 = norm(h1)
+        first = n1 * vec(0) + vec(1)
+        fl = first.astype(BF16)
+        inner = lambda g: nn(fl[:, window(g) : window(g) + 256], w1_s[g]) + vec(8 + g)
+        active, slope, branch = [], [], []
+        ahead = inner(0)
+        for g in range(4):
+            now, ahead = ahead, (inner(g + 1) if g < 3 else None)
+            a, sl = gelu_parts(now)
+            active.append(a.astype(BF16))
+            slope.append(sl)
+            branch.append(nt(active[g], w2_s[g]))
+        h2 = first + (join(branch) + vec(7))
+        n2, inv2 = norm(h2)
+        reuse(row, (5, 6, 7))
+        out_s[...] = (n2 * vec(2) + vec(3)).astype(BF16)
+        out_copies(row, (5,))[0].start()
+        dy = cot_ref[row].astype(F32)
+        dh2 = norm_back(dy, n2, inv2, vec(2))
+        dbl = dh2.astype(BF16)
+        dbt = dbl.T
+        flt = fl.T
+        ones = jnp.ones((16, seq), BF16)
+        dfirst = []
+        gb = []
+        for g in range(4):
+            da = nn(dbl[:, window(g) : window(g) + 256], w2_s[g])
+            di = (da * slope[g]).astype(BF16)
+            dfirst.append(nt(di, w1_s[g]))
+            g2 = nn(dbt[192 * g : 192 * g + 192, :], active[g])
+            ext = nn(jnp.concatenate([flt[192 * g : 192 * g + 192, :], ones], axis=0), di)
+            for half, base in enumerate(group_rows(owned, g)):
+                add_blocks(s2_ref, base, g2[:, 384 * half : 384 * half + 384])
+                add_blocks(s1_ref, base, ext[:192, 384 * half : 384 * half + 384])
+            gb.append(ext[192:193])
+        df = dh2 + join(dfirst)
+        dh1 = norm_back(df, n1, inv1, vec(0))
+        dat = dh1.astype(BF16)
+        res_s[...] = dat
+        out_copies(row, (6,))[0].start()
+        go = nn(ct_s[row], dat)
+        for q in range(4):
+            add_blocks(so_ref, 1152 * q, go[192 * q : 192 * q + 192])
+        dct_s[...] = nt(wo_s[...], dat).astype(BF16)
+        out_copies(row, (7,))[0].start()
+        z = jnp.zeros((1, dy.shape[1]), F32)
+        gv_ref[...] += jnp.concatenate(
+            [col_sum(df * n1), col_sum(df), col_sum(dy * n2), col_sum(dy), z, z, col_sum(dat.astype(F32)), col_sum(dbl.astype(F32))] + gb, axis=0)
+        return carry
+
+    lax.fori_loop(0, n_rows, feed_forward, 0)
+    for copy in out_copies(n_rows - 1, range(8)):
+        copy.wait()
+
+
+def front(p, owned, sum_rows, lengths, tokens, cot, wq, wo, w1, w2, vec, mo, m1, m2, ident):
     n, seq, d = tokens.shape
     slim, tall = wq.shape[1:]
     up = lambda r, m: -(-r // m) * m
     qrows = up(3 * tall, 32)
-    rrows = up(3 * fold_rows(4 * slim, 4 * tall), 32)
+    rrows = up(3 * fold_rows(4 * slim, 4 * tall), 16)
     count = gather_copies(p)
     hbm = pl.BlockSpec(memory_space=pl.ANY)
     act = lambda a, b: jax.ShapeDtypeStruct((n, a, b), BF16)
+    tm, mt = pltpu.VMEM((seq, d), BF16), pltpu.VMEM((d, seq), BF16)
     return pl.pallas_call(
-        functools.partial(open_kernel, p),
-        out_shape=[act(d, seq), act(seq, d), act(d, seq), act(seq, d), act(d, seq), jax.ShapeDtypeStruct((n, 16, seq), F32)]
-        + [jax.ShapeDtypeStruct((4, 256, 768), BF16)] * 2
-        + [jax.ShapeDtypeStruct((768, 768), BF16), jax.ShapeDtypeStruct((4, 192, 576), BF16)],
-        in_specs=[pl.BlockSpec(memory_space=pltpu.SMEM)] + [VMEM] * 6,
-        out_specs=[hbm] * 5 + [VMEM] * 5,
+        functools.partial(front_kernel, p, owned),
+        out_shape=[act(d, seq), act(seq, d), act(d, seq), act(seq, d), act(d, seq), act(seq, d), act(seq, d), act(d, seq)]
+        + [jax.ShapeDtypeStruct((n, 16, seq), F32), jax.ShapeDtypeStruct((4, 192, 576), BF16)]
+        + [jax.ShapeDtypeStruct((sum_rows, 128), BF16)] * 3
+        + [jax.ShapeDtypeStruct((12, 768), F32)],
+        in_specs=[pl.BlockSpec(memory_space=pltpu.SMEM)] + [VMEM] * 10,
+        out_specs=[hbm] * 8 + [VMEM] * 6,
         scratch_shapes=[
             pltpu.VMEM((p.Z, p.C, p.X, p.Y, qrows, 128), BF16),
             pltpu.VMEM((p.Z, p.C, p.X, p.Y, rrows, 128), BF16),
+            pltpu.VMEM((p.Z * p.X // 2, 256, 1024), BF16),
             pltpu.VMEM((3, 4, 256, 256), BF16),
-            pltpu.VMEM((n, d, seq), BF16), pltpu.VMEM((n, seq, d), BF16), pltpu.VMEM((n, d, seq), BF16), pltpu.VMEM((n, seq, d), BF16), pltpu.VMEM((n, d, seq), BF16),
-            pltpu.VMEM((d, seq), BF16), pltpu.VMEM((seq, seq), F32), pltpu.VMEM((d, 8), F32),
+            mt, tm, mt, tm, pltpu.VMEM((n, d, seq), BF16),
+            mt, pltpu.VMEM((seq, seq), F32), pltpu.VMEM((d, 8), F32),
+            pltpu.VMEM((4, 256, 768), BF16), pltpu.VMEM((4, 256, 768), BF16), pltpu.VMEM((768, 768), BF16),
+            tm, tm, mt,
             pltpu.SemaphoreType.DMA((count,)), pltpu.SemaphoreType.DMA((count,)),
             pltpu.SemaphoreType.DMA((count,)), pltpu.SemaphoreType.DMA((count,)),
-            pltpu.SemaphoreType.DMA((n, 5)),
+            pltpu.SemaphoreType.DMA((8,)),
         ],
-        compiler_params=pltpu.CompilerParams(collective_id=ident, has_side_effects=True, vmem_limit_bytes=60 * 2**20),
-    )(lengths, tokens, wq, wo, w1, w2, vec)
+        compiler_params=pltpu.CompilerParams(collective_id=ident, has_side_effects=True, vmem_limit_bytes=62 * 2**20),
+    )(lengths, tokens, cot, wq, wo, w1, w2, vec, mo, m1, m2)
 
 
 def on_diagonal(n):
@@ -1074,14 +1078,18 @@
     return jnp.where(r < 192, channel - base, -1000), s
 
 
+def paced(o, f1, f2):
+    return ((5, o[2]), (7, f1[1]), (10, o[3]), (10, f2[1]), (13, f1[2]), (16, o[4]), (16, f2[2]), (19, f1[3]), (22, o[5]), (23, f2[3]))
+
+
 def owner_kernel(p, shares, *refs):
-    (len_ref, wt_ref, so_ref, s1_ref, s2_ref, gv_ref, gmq_ref, wq_ref, wo_ref, w1_ref, w2_ref, vec_ref, vm1_ref, vm2_ref,
+    (len_ref, wt_ref, so_hbm, s1_hbm, s2_hbm, gv_ref, gmq_ref, wq_ref, wo_ref, w1_ref, w2_ref, vec_ref, vm1_ref, vm2_ref,
      x_hbm, qt_hbm, k_hbm, kt_hbm, v_hbm, ct_hbm, lse_ref, dct_hbm, res_hbm,
      gt_ref, mq_ref, mo_ref, m1_ref, m2_ref, nq_ref, no_ref, n1_ref, n2_ref, f_ref, s_ref, v_ref,
-     x_s, qt_s, k_s, kt_s, v_s, ct_s, dct_s, res_s, bias_s, dq_s, dk_s, dv_s, gq_s, gv2_s, sq_s, oo_s,
+     so_ref, s1_ref, s2_ref, x_s, qt_s, k_s, kt_s, v_s, ct_s, dct_s, res_s, bias_s, dq_s, dk_s, dv_s, gq_s, gv2_s, sq_s, oo_s,
      yo_s, yf_s, yq_s, xo_s, xo_r, tmf_s, txf_s, tmq_s, txq_s, tv_s, rmf_s, rxf_s, rmq_s, rxq_s, rv_s,
-     in_sem, x_send, x_recv) = refs[: 35 + 34]
-    rest = refs[35 + 34 :]
+     in_sem, src_sem, x_send, x_recv) = refs[: 35 + 38]
+    rest = refs[35 + 38 :]
     p.locate()
     p.greet(corner=True)
     d, n = lax.axis_index("dp"), lax.axis_index("narrow")
@@ -1092,7 +1100,10 @@
     def loads(row):
         return [pltpu.make_async_copy(src.at[row], dst.at[row], in_sem.at[row, i]) for i, (src, dst) in enumerate(pairs)]
 
-    for row in range(n_rows):
+    sources = [pltpu.make_async_copy(a, b, src_sem.at[i]) for i, (a, b) in enumerate(((so_hbm, so_ref), (s1_hbm, s1_ref), (s2_hbm, s2_ref)))]
+    for copy in sources[:1] + loads(0) + sources[1:]:
+        copy.start()
+    for row in range(1, n_rows):
         for copy in loads(row):
             copy.start()
     o = sum_steps(p, shares[0], so_ref, oo_s, rest[:10])
@@ -1102,10 +1113,10 @@
     q_all = rest[36]
     f1_half, f1_other, f2_half, f2_other = rest[15], rest[16], rest[24], rest[25]
     p.meet(corner=True)
-    for step in (o[0], f1[0], f2[0]):
-        step()
+    sources[0].wait()
+    o[0]()
     turns = [[] for _ in range(12 * n_rows)]
-    for i, step in ((0, f1[1]), (5, o[2]), (6, f2[1]), (9, f1[2]), (10, o[3]), (14, f2[2]), (14, f1[3]), (16, o[4]), (18, f2[3]), (22, f1[4]), (23, o[5])):
+    for i, step in paced(o, f1, f2):
         turns[i * n_rows // 2].append(step)
     gq_s[...] = jnp.zeros_like(gq_s)
     gv2_s[...] = jnp.zeros_like(gv2_s)
@@ -1119,7 +1130,11 @@
 
         @pl.when(row == 0)
         def _():
+            for copy in sources[1:]:
+                copy.wait()
             o[1]()
+            f1[0]()
+            f2[0]()
 
         def pair(j, carry):
             lo = pl.multiple_of(128 * j, 128)
@@ -1238,7 +1253,7 @@
     @pl.when(core0)
     def _():
         q_give()
-        for step in (lambda: grad_in(0), o[6], f2[4], lambda: grad_in(1), f1[5], f2[5], o[7], o[8], f1[6], f2[6]):
+        for step in (lambda: grad_in(0), o[6], f1[4], f2[4], lambda: grad_in(1), f1[5], o[7], f2[5], o[8], f1[6], f2[6]):
             step()
         yo_s[...] = ns_start([wide_rows(oo_s, 0, 4).astype(F32)])[0]
 
@@ -1254,7 +1269,7 @@
 
     @pl.when(core1)
     def _():
-        for step in (q[0], o[6], f2[4], lambda: grad_in(0), q[1], lambda: grad_in(1), f1[5], f2[5], o[7], o[8], q[2], f1[6], f2[6]):
+        for step in (q[0], o[6], f1[4], f2[4], lambda: grad_in(0), q[1], lambda: grad_in(1), f1[5], o[7], f2[5], o[8], q[2], f1[6], f2[6]):
             step()
         for i, y in enumerate(ns_start([blocks(a, b).astype(F32) for a, b in ((f1_other, f1_half), (f2_other, f2_half))])):
             yf_s[i] = y
@@ -1375,7 +1390,8 @@
     outs = [jax.ShapeDtypeStruct(tokens.shape, BF16)] + [shape(w) for w in weights] * 2 + [shape(vec)] * 3
     hbm = pl.BlockSpec(memory_space=pl.ANY)
     tm, mt = pltpu.VMEM((n, seq, d), BF16), pltpu.VMEM((n, d, seq), BF16)
-    scratch = [tm, mt, tm, mt, tm, mt, mt, pltpu.VMEM((n, seq, d), BF16), pltpu.VMEM((seq, seq), F32)]
+    scratch = [pltpu.VMEM((4608, 128), BF16)] * 3
+    scratch += [tm, mt, tm, mt, tm, mt, mt, pltpu.VMEM((n, seq, d), BF16), pltpu.VMEM((seq, seq), F32)]
     scratch += [mt] * 3 + [pltpu.VMEM((3, 192, 768), F32), pltpu.VMEM((8, 768), F32)]
     scratch += [pltpu.VMEM((shares[3].rows, 128), BF16), pltpu.VMEM((shares[0].rows, 128), BF16)]
     scratch += [pltpu.VMEM((768, 768), F32), pltpu.VMEM((2, 192, 768), F32), pltpu.VMEM((3, 192, 256), F32)]
@@ -1383,14 +1399,14 @@
     to_f, to_q, to_v = (2 * slim, 384), (96, 128), (32, 128)
     scratch += [pltpu.VMEM((2, 2) + k, BF16) for k in (to_f, to_f, to_q, to_q, to_v)]
     scratch += [pltpu.VMEM((4,) + k, BF16) for k in (to_f, to_f, to_q, to_q, to_v)]
-    scratch += [pltpu.SemaphoreType.DMA((n, 8)), pltpu.SemaphoreType.DMA((24,)), pltpu.SemaphoreType.DMA((24,))]
+    scratch += [pltpu.SemaphoreType.DMA((n, 8)), pltpu.SemaphoreType.DMA((3,)), pltpu.SemaphoreType.DMA((24,)), pltpu.SemaphoreType.DMA((24,))]
     scratch += shares[0].scratch(p)
     for s in shares[1:]:
         scratch += s.scratch()
     return pl.pallas_call(
         functools.partial(owner_kernel, p, shares),
         out_shape=outs,
-        in_specs=[pl.BlockSpec(memory_space=pltpu.SMEM)] + [VMEM] * 13 + [hbm] * 6 + [VMEM] + [hbm] * 2,
+        in_specs=[pl.BlockSpec(memory_space=pltpu.SMEM), VMEM] + [hbm] * 3 + [VMEM] * 9 + [hbm] * 6 + [VMEM] + [hbm] * 2,
         out_specs=[VMEM] * 12,
         scratch_shapes=scratch,
         compiler_params=pltpu.CompilerParams(collective_id=ident, has_side_effects=True, vmem_limit_bytes=62 * 2**20),
@@ -1423,11 +1439,12 @@
         shares = [Shares(p, 4608), Owned(p, 576), Owned(p, 576), Solo(p, 448)]
     else:
         shares = [Shares(p, r) for r in (4608, 4608, 4608, 3456 + 72)]
-    qt, k, kt, v, ct, lse, w1p, w2p, wot, wt = opening(p, doc_lengths, tokens, wq, out_weight, w1, w2, vectors, 0)
-    out_act, res, dct, so, s1, s2, gv = ffn(tokens, cotangent, ct, w1p, w2p, wot, vectors, out_moment, m1, m2, shares[0].rows, owned)
+    qt, k, kt, v, ct, out_act, res, dct, lse, wt, so, s1, s2, gv = front(
+        p, owned, shares[0].rows, doc_lengths, tokens, cotangent, wq, out_weight, w1, w2, vectors, out_moment, m1, m2, 0)
     acts = (tokens, qt, k, kt, v, ct, lse, dct, res)
-    gt, gq, go, g1, g2, nq, no, n1, n2, f, s, vn = hand_over((closing_owned if owned else closing)(
-        p, shares, doc_lengths, wt, so, s1, s2, gv, mq, (wq, out_weight, w1, w2), vectors, vec_moment1, vec_moment2, acts, 1))
+    rest = (closing_owned if owned else closing)(
+        p, shares, doc_lengths, wt, so, s1, s2, gv, mq, (wq, out_weight, w1, w2), vectors, vec_moment1, vec_moment2, acts, 1)
+    out_act, gt, gq, go, g1, g2, nq, no, n1, n2, f, s, vn = hand_over([out_act] + list(rest))
     return (out_act, gt, flip(gq), go, flip(g1), flip(g2), flip(nq), no, flip(n1), flip(n2), f, s, vn)
 
 

time: 168 us -> 157 us (0.935)
  Pallas kernels: 168 us -> 156 us
    pallas_call x2 -> x1, Pallas kernels: 95 us -> 81.7 us  [front(): pl.pallas_call(functools.partial(front_kernel, p, owned), out_shape=[act(...]
where the time goes in v2:
time: 157 us
  Pallas kernels  156 us (99%)
    pallas_call x1, Pallas kernels, front(): pl.pallas_call(functools.partial(front_kernel, p, owned), out_shape=[act(...  81.7 us
    pallas_call x1, Pallas kernels, closing_owned(): pl.pallas_call(functools.partial(owner_kernel, p, shares), out_shape=outs...  70.1 us
    pallas_call x1, Pallas kernels, hand_over(): pl.pallas_call(hand_over_kernel, out_shape=[jax.ShapeDtypeStruct(a.shape,...  4.2 us

profile of v2, /device:TPU:0, one launch (start us, length us, event | category | flops | bytes accessed | tf_op | source)
XLA Modules:
  0.0 156.9 jit_solution(9510191692031515368)
XLA Ops:
  0.6 81.7 %shard_map.237 = (bf16[2,768,512]{2,1,0:T(8,128)(2,1)}, bf16[2,512,768]{2,1,0:T(8,128)(2,1)}, bf16[2,768,512]{2,1,0:T(8,128)(2,1)}, bf16[2,512,768]{2,1,0:T(8,12...) custom-call(s32[2,4]{1,0:T(2,128)} %refs_0_.1, ...), custom_call_target="tpu_custom_call" | custom-call | tf_op jit(solution)/shard_map/pallas_call | solution.py:641
  82.4 70.1 %shard_map.238 = (bf16[2,512,768]{2,1,0:T(8,128)(2,1)}, f32[12,24,48]{2,1,0:T(8,128)}, f32[1,192,96]{2,1,0:T(8,128)}, f32[4,24,192]{2,1,0:T(8,128)}, f32[4,24,19...) custom-call(s32[2,4]{1,0:T(2,128)} %refs_0_.1, ...), custom_call_target="tpu_custom_call" | custom-call | tf_op jit(solution)/shard_map/pallas_call | solution.py:1406
  152.5 4.2 %shard_map.239 = (bf16[2,512,768]{2,1,0:T(8,128)(2,1)}, bf16[2,512,768]{2,1,0:T(8,128)(2,1)}, f32[12,24,48]{2,1,0:T(8,128)}, f32[1,192,96]{2,1,0:T(8,128)}, f32[...) custom-call(bf16[2,512,768]{2,1,0:T(8,128)(2,1)} %get-tuple-element., ...), custom_call_target="tpu_custom_call" | custom-call | tf_op jit(solution)/shard_map/pallas_call | solution.py:1423

commit v3 on v2

--- a/solution.py
+++ b/solution.py
@@ -671,21 +671,28 @@
     return [y * (1.0 / (jnp.sqrt(jnp.sum(y * y)) + 1e-07)) for y in values]
 
 
-def ns_poly(values):
-    n = values[0].shape[0]
-    diag = on_diagonal(n)
+def ns_shift(t):
+    return jnp.where(t >= 3, 0.8, jnp.where(t == 2, 0.5, 0.0)).astype(F32)
+
+
+def ns_poly(values, m):
+    diag = on_diagonal(values[0].shape[0])
     lows = [y.astype(BF16) for y in values]
     grams = [nt(l, l) for l in lows]
-    mids = [jnp.sum(jnp.where(diag, g, 0.0)) * (1.0 / n) for g in grams]
-    rest = [jnp.where(diag, g - m, g) for g, m in zip(grams, mids)]
+    rest = [jnp.where(diag, g - m, g) for g in grams]
     lowr = [r.astype(BF16) for r in rest]
     squares = [nn(r, r) for r in lowr]
-    return mids, [((ns_second + 2.0 * ns_third * m) * r + ns_third * s).astype(BF16) for m, r, s in zip(mids, rest, squares)]
-
-
-def ns_step(values, mids, polys):
+    return [((ns_second + 2.0 * ns_third * m) * r + ns_third * s).astype(BF16) for r, s in zip(rest, squares)]
+
+
+def ns_step(values, m, polys):
     moved = [nn(q, y.astype(BF16)) for q, y in zip(polys, values)]
-    return [(ns_first + ns_second * m + ns_third * m * m) * y + t for m, y, t in zip(mids, values, moved)]
+    return [(ns_first + ns_second * m + ns_third * m * m) * y + t for y, t in zip(values, moved)]
+
+
+def ns_sweep(values, t):
+    m = ns_shift(t)
+    return ns_step(values, m, ns_poly(values, m))
 
 
 def close_kernel(p, shares, *refs):
@@ -693,8 +700,8 @@
      x_hbm, qt_hbm, k_hbm, kt_hbm, v_hbm, ct_hbm, lse_ref, dct_hbm, res_hbm,
      gt_ref, mq_ref, mo_ref, m1_ref, m2_ref, nq_ref, no_ref, n1_ref, n2_ref, f_ref, s_ref, v_ref,
      x_s, qt_s, k_s, kt_s, v_s, ct_s, dct_s, res_s, bias_s, dq_s, dk_s, dv_s, gq_s, gv2_s, sq_s, oo_s, o1_s, o2_s, oq_s,
-     y_s, po_s, pf_s, mid_s, xo_s, xf_s, xq_s, xo_r, xf_r, xq_r, in_sem, x_send, x_recv) = refs[: 35 + 32]
-    rest = refs[35 + 32 :]
+     y_s, po_s, pf_s, xo_s, xf_s, xq_s, xo_r, xf_r, xq_r, in_sem, x_send, x_recv) = refs[: 35 + 31]
+    rest = refs[35 + 31 :]
     p.locate()
     d, n = lax.axis_index("dp"), lax.axis_index("narrow")
     n_rows, seq = x_s.shape[:2]
@@ -800,26 +807,22 @@
 
         @pl.when(on0)
         def _():
-            mids, polys = ns_poly([y_s[0:768, :]])
-            mid_s[0:1, :] = jnp.broadcast_to(mids[0], (1, 128))
-            po_s[...] = polys[0]
+            po_s[...] = ns_poly([y_s[0:768, :]], ns_shift(t))[0]
 
         @pl.when(on1)
         def _():
-            mids, polys = ns_poly(eight())
-            for i in range(8):
-                mid_s[i : i + 1, :] = jnp.broadcast_to(mids[i], (1, 128))
-                pf_s[i] = polys[i]
+            for i, poly in enumerate(ns_poly(eight(), ns_shift(t - late))):
+                pf_s[i] = poly
 
         at_turn(t, before)
 
         @pl.when(on0)
         def _():
-            y_s[0:768, :] = ns_step([y_s[0:768, :]], [mid_s[0:1, 0:1]], [po_s[...]])[0]
+            y_s[0:768, :] = ns_step([y_s[0:768, :]], ns_shift(t), [po_s[...]])[0]
 
         @pl.when(on1)
         def _():
-            for i, y in enumerate(ns_step(eight(), [mid_s[i : i + 1, 0:1] for i in range(8)], [pf_s[i] for i in range(8)])):
+            for i, y in enumerate(ns_step(eight(), ns_shift(t - late), [pf_s[i] for i in range(8)])):
                 y_s[192 * i : 192 * i + 192, :] = y
 
         at_turn(t, between)
@@ -853,7 +856,7 @@
 
         def turn(t, carry):
             ys = [y_s[192 * i : 192 * i + 192, :256] for i in range(6)]
-            for i, y in enumerate(ns_step(ys, *ns_poly(ys))):
+            for i, y in enumerate(ns_sweep(ys, t)):
                 y_s[192 * i : 192 * i + 192, :256] = y
             return carry
 
@@ -923,7 +926,7 @@
     scratch = [tm, mt, tm, mt, tm, mt, mt, pltpu.VMEM((n, seq, d), BF16), pltpu.VMEM((seq, seq), F32)]
     scratch += [pltpu.VMEM((d, seq), BF16)] * 3 + [pltpu.VMEM((3, 192, 768), F32), pltpu.VMEM((8, 768), F32)]
     scratch += [flat(shares[3].rows)] + [flat(s.rows) for s in shares]
-    scratch += [pltpu.VMEM((1536, 768), F32), pltpu.VMEM((768, 768), BF16), pltpu.VMEM((8, 192, 192), BF16), pltpu.VMEM((8, 128), F32)]
+    scratch += [pltpu.VMEM((1536, 768), F32), pltpu.VMEM((768, 768), BF16), pltpu.VMEM((8, 192, 192), BF16)]
     scratch += [pltpu.VMEM((4 * slim, 768), BF16), pltpu.VMEM((8 * slim, 768), BF16), pltpu.VMEM((576, 128), BF16)] * 2
     scratch += [pltpu.SemaphoreType.DMA((n, 8)), pltpu.SemaphoreType.DMA((3,)), pltpu.SemaphoreType.DMA((3,))]
     for s in shares:
@@ -1112,14 +1115,20 @@
     q_give, q_gave, q = solo_steps(p, shares[3], sq_s, rest[28:39])
     q_all = rest[36]
     f1_half, f1_other, f2_half, f2_other = rest[15], rest[16], rest[24], rest[25]
+    turns = [[] for _ in range(12 * n_rows)]
+    for i, step in paced(o, f1, f2):
+        turns[i * n_rows // 2].append(step)
+    slim, tall = gmq_ref.shape[1:]
+    up = hot((192, tall), 0, n * tall)
+    for c in range(3):
+        held = jnp.zeros((tall, 768), F32)
+        for g in range(4):
+            held = held + tn((0.95 * gmq_ref[4 * c + g]).astype(BF16), hot((slim, 768), 192 * g + d * slim, 0))
+        gq_s[c] = nn(up, held.astype(BF16))
+    gv2_s[...] = jnp.zeros_like(gv2_s)
     p.meet(corner=True)
     sources[0].wait()
     o[0]()
-    turns = [[] for _ in range(12 * n_rows)]
-    for i, step in paced(o, f1, f2):
-        turns[i * n_rows // 2].append(step)
-    gq_s[...] = jnp.zeros_like(gq_s)
-    gv2_s[...] = jnp.zeros_like(gv2_s)
     lane = lax.broadcasted_iota(jnp.int32, (192, 256), 1)
 
     def one_row(row, carry):
@@ -1169,15 +1178,8 @@
         return carry
 
     lax.fori_loop(0, n_rows, one_row, 0)
-    slim, tall = gmq_ref.shape[1:]
     half = shares[3].half
-    up = hot((192, tall), 0, n * tall)
-    values = []
-    for c in range(3):
-        held = jnp.zeros((tall, 768), F32)
-        for g in range(4):
-            held = held + tn((0.95 * gmq_ref[4 * c + g]).astype(BF16), hot((slim, 768), 192 * g + d * slim, 0))
-        values.append(gq_s[c] + nn(up, held.astype(BF16)))
+    values = [gq_s[c] for c in range(3)]
     gv = jnp.concatenate([gv_ref[0:4], gv2_s[0:2], gv_ref[6:12]], axis=0)
     lane = lax.broadcasted_iota(jnp.int32, (192, 128), 1)
     for g in range(4):
@@ -1259,7 +1261,7 @@
 
         def turn(t, carry):
             y = yo_s[...]
-            yo_s[...] = ns_step([y], *ns_poly([y]))[0]
+            yo_s[...] = ns_sweep([y], t)[0]
             return carry
 
         lax.fori_loop(0, NS_STEPS, turn, 0)
@@ -1276,7 +1278,7 @@
 
         def f_turn(t, carry):
             ys = [yf_s[i] for i in range(2)]
-            for i, y in enumerate(ns_step(ys, *ns_poly(ys))):
+            for i, y in enumerate(ns_sweep(ys, t)):
                 yf_s[i] = y
             return carry
 
@@ -1300,7 +1302,7 @@
 
         def turn(t, carry):
             ys = [yq_s[i] for i in range(3)]
-            for i, y in enumerate(ns_step(ys, *ns_poly(ys))):
+            for i, y in enumerate(ns_sweep(ys, t)):
                 yq_s[i] = y
             return carry
 
@@ -1413,18 +1415,29 @@
     )(lengths, wt, so, s1, s2, gv, mq, *weights, vec, vm1, vm2, *acts)
 
 
-def hand_over_kernel(*refs):
-    half = len(refs) // 2
-    for src, dst in zip(refs[:half], refs[half:]):
-        dst[...] = src[...]
+def hand_over_kernel(count, *refs):
+    src, dst, held = refs[:count], refs[count : 2 * count], refs[2 * count : 3 * count]
+    here, away = refs[3 * count :]
+    loads = [pltpu.make_async_copy(src[i], held[i], here.at[i]) for i in range(count)]
+    stores = [pltpu.make_async_copy(held[i], dst[i], away.at[i]) for i in range(count)]
+    for load in loads:
+        load.start()
+    for load, store in zip(loads, stores):
+        load.wait()
+        store.start()
+    for store in stores:
+        store.wait()
 
 
 def hand_over(values):
+    hbm = pl.BlockSpec(memory_space=pl.ANY)
+    count = len(values)
     return pl.pallas_call(
-        hand_over_kernel,
+        functools.partial(hand_over_kernel, count),
         out_shape=[jax.ShapeDtypeStruct(a.shape, a.dtype) for a in values],
-        in_specs=[VMEM] * len(values),
-        out_specs=[VMEM] * len(values),
+        in_specs=[hbm] * count,
+        out_specs=[hbm] * count,
+        scratch_shapes=[pltpu.VMEM(a.shape, a.dtype) for a in values] + [pltpu.SemaphoreType.DMA((count,))] * 2,
         compiler_params=pltpu.CompilerParams(vmem_limit_bytes=60 * 2**20),
     )(*values)
 

time: 157 us -> 155 us (0.987)
  Pallas kernels: 156 us -> 153 us
    pallas_call x1, Pallas kernels: 70.1 us -> 68.3 us  [closing_owned(): pl.pallas_call(functools.partial(owner_kernel, p, shares), out_shape=outs...]
where the time goes in v3:
time: 155 us; the launch traced here: 154 us
  Pallas kernels  153 us (99%)
    pallas_call x1, Pallas kernels, front(): pl.pallas_call(functools.partial(front_kernel, p, owned), out_shape=[act(...  81.3 us
    pallas_call x1, Pallas kernels, closing_owned(): pl.pallas_call(functools.partial(owner_kernel, p, shares), out_shape=outs...  68.3 us
    pallas_call x1, Pallas kernels, hand_over(): pl.pallas_call(functools.partial(hand_over_kernel, count), out_shape=[jax...  3.63 us

profile of v3, /device:TPU:0, one launch (start us, length us, event | category | flops | bytes accessed | tf_op | source)
XLA Modules:
  0.0 154.1 jit_solution(16150150810049573933)
XLA Ops:
  0.6 81.3 %shard_map.237 = (bf16[2,768,512]{2,1,0:T(8,128)(2,1)}, bf16[2,512,768]{2,1,0:T(8,128)(2,1)}, bf16[2,768,512]{2,1,0:T(8,128)(2,1)}, bf16[2,512,768]{2,1,0:T(8,12...) custom-call(s32[2,4]{1,0:T(2,128)} %refs_0_.1, ...), custom_call_target="tpu_custom_call" | custom-call | tf_op jit(solution)/shard_map/pallas_call | solution.py:641
  82.0 68.3 %shard_map.238 = (bf16[2,512,768]{2,1,0:T(8,128)(2,1)}, f32[12,24,48]{2,1,0:T(8,128)}, f32[1,192,96]{2,1,0:T(8,128)}, f32[4,24,192]{2,1,0:T(8,128)}, f32[4,24,19...) custom-call(s32[2,4]{1,0:T(2,128)} %refs_0_.1, ...), custom_call_target="tpu_custom_call" | custom-call | tf_op jit(solution)/shard_map/pallas_call | solution.py:1408
  150.3 3.6 %shard_map.239 = (bf16[2,512,768]{2,1,0:T(8,128)(2,1)}, bf16[2,512,768]{2,1,0:T(8,128)(2,1)}, f32[12,24,48]{2,1,0:T(8,128)}, f32[1,192,96]{2,1,0:T(8,128)}, f32[...) custom-call(bf16[2,512,768]{2,1,0:T(8,128)(2,1)} %get-tuple-element., ...), custom_call_target="tpu_custom_call" | custom-call | tf_op jit(solution)/shard_map/pallas_call | solution.py:1435

commit v4 on v3

--- a/solution.py
+++ b/solution.py
@@ -476,7 +476,7 @@
         for steps, at in ((q_own, t), (q_on, t - 1), (q_over, t - (1 if owned else 2))):
             if 0 <= at < len(steps):
                 steps[at]()
-        if t == p.Z - 2:
+        if t == p.Z - 3:
             r_z()
     r_own[0]()
     q_done()
@@ -671,15 +671,28 @@
     return [y * (1.0 / (jnp.sqrt(jnp.sum(y * y)) + 1e-07)) for y in values]
 
 
+def less_diagonal(g, m):
+    n = g.shape[0]
+    if n % 128:
+        return jnp.where(on_diagonal(n), g - m, g)
+    unit = jnp.where(on_diagonal(128), m, 0.0)
+    rows = []
+    for i in range(n // 128):
+        row = g[128 * i : 128 * i + 128, :]
+        tiles = [row[:, 128 * j : 128 * j + 128] for j in range(n // 128)]
+        tiles[i] = tiles[i] - unit
+        rows.append(jnp.concatenate(tiles, axis=1))
+    return jnp.concatenate(rows, axis=0)
+
+
 def ns_shift(t):
     return jnp.where(t >= 3, 0.8, jnp.where(t == 2, 0.5, 0.0)).astype(F32)
 
 
 def ns_poly(values, m):
-    diag = on_diagonal(values[0].shape[0])
     lows = [y.astype(BF16) for y in values]
     grams = [nt(l, l) for l in lows]
-    rest = [jnp.where(diag, g - m, g) for g in grams]
+    rest = [less_diagonal(g, m) for g in grams]
     lowr = [r.astype(BF16) for r in rest]
     squares = [nn(r, r) for r in lowr]
     return [((ns_second + 2.0 * ns_third * m) * r + ns_third * s).astype(BF16) for r, s in zip(rest, squares)]
@@ -1090,9 +1103,9 @@
      x_hbm, qt_hbm, k_hbm, kt_hbm, v_hbm, ct_hbm, lse_ref, dct_hbm, res_hbm,
      gt_ref, mq_ref, mo_ref, m1_ref, m2_ref, nq_ref, no_ref, n1_ref, n2_ref, f_ref, s_ref, v_ref,
      so_ref, s1_ref, s2_ref, x_s, qt_s, k_s, kt_s, v_s, ct_s, dct_s, res_s, bias_s, dq_s, dk_s, dv_s, gq_s, gv2_s, sq_s, oo_s,
-     yo_s, yf_s, yq_s, xo_s, xo_r, tmf_s, txf_s, tmq_s, txq_s, tv_s, rmf_s, rxf_s, rmq_s, rxq_s, rv_s,
-     in_sem, src_sem, x_send, x_recv) = refs[: 35 + 38]
-    rest = refs[35 + 38 :]
+     yo_s, yf_s, yq_s, xo_s, xo_r, tmf_s, txf_s, tmq_s, txq_s, tv_s, rmf_s, rxf_s, rmq_s, rxq_s, rv_s, sel_s,
+     in_sem, src_sem, x_send, x_recv) = refs[: 35 + 39]
+    rest = refs[35 + 39 :]
     p.locate()
     p.greet(corner=True)
     d, n = lax.axis_index("dp"), lax.axis_index("narrow")
@@ -1100,8 +1113,11 @@
     n_rows, seq = x_s.shape[:2]
     pairs = ((qt_hbm, qt_s), (k_hbm, k_s), (dct_hbm, dct_s), (v_hbm, v_s), (ct_hbm, ct_s), (kt_hbm, kt_s), (x_hbm, x_s), (res_hbm, res_s))
 
-    def loads(row):
-        return [pltpu.make_async_copy(src.at[row], dst.at[row], in_sem.at[row, i]) for i, (src, dst) in enumerate(pairs)]
+    def load(row, i):
+        return pltpu.make_async_copy(pairs[i][0].at[row], pairs[i][1].at[row], in_sem.at[row, i])
+
+    def loads(row, count=8):
+        return [load(row, i) for i in range(count)]
 
     sources = [pltpu.make_async_copy(a, b, src_sem.at[i]) for i, (a, b) in enumerate(((so_hbm, so_ref), (s1_hbm, s1_ref), (s2_hbm, s2_ref)))]
     for copy in sources[:1] + loads(0) + sources[1:]:
@@ -1126,6 +1142,10 @@
             held = held + tn((0.95 * gmq_ref[4 * c + g]).astype(BF16), hot((slim, 768), 192 * g + d * slim, 0))
         gq_s[c] = nn(up, held.astype(BF16))
     gv2_s[...] = jnp.zeros_like(gv2_s)
+    for x in range(2):
+        for c in range(3):
+            at, lane_of = canon(p.y == 1, (p.z * 2 + x) * slim)
+            sel_s[x, c] = jnp.logical_and(jnp.logical_and(at >= 0, at < slim), at + c * slim == lane_of).astype(BF16)
     p.meet(corner=True)
     sources[0].wait()
     o[0]()
@@ -1134,7 +1154,7 @@
     def one_row(row, carry):
         same = ids(len_ref, row, (seq, seq), 0) == ids(len_ref, row, (seq, seq), 1)
         bias_s[...] = jnp.where(same, 0.0, -1e30)
-        for copy in loads(row):
+        for copy in loads(row, 6):
             copy.wait()
 
         @pl.when(row == 0)
@@ -1165,6 +1185,7 @@
             return carry
 
         lax.fori_loop(0, 6, pair, 0)
+        load(row, 6).wait()
         for g in range(4):
             lo = window(g)
             r = slice(192 * g, 192 * g + 192)
@@ -1208,11 +1229,11 @@
         for g in range(4):
             r = slice(192 * g, 192 * g + 192)
             dx.append(nn(wt_ref[g], jnp.concatenate([dq_s[row, r, :], dk_s[row, r, :], dv_s[row, r, :]], axis=0)))
+        load(row, 7).wait()
         gt_ref[row] = (res_s[row].astype(F32) + jnp.concatenate(dx, axis=0).T).astype(BF16)
 
     wires = Wires(p, x_send, x_recv)
     me = 2 * p.x + p.y
-    odd = lax.rem(me, 2) == 1
     around = ((1, 0), (0, 1), (1, 1))
 
     def scatter(src, dst, cores=(1,)):
@@ -1246,9 +1267,7 @@
         for x in range(2):
             part = jnp.zeros((192, 128), F32)
             for c, m in enumerate(three):
-                at, s = canon(odd, (p.z * 2 + x) * slim)
-                sel = jnp.logical_and(jnp.logical_and(at >= 0, at < slim), at + c * slim == s).astype(BF16)
-                part = part + nn(m, sel)
+                part = part + nn(m, sel_s[x, c])
             for y in range(2):
                 dst[x, y] = part[96 * y : 96 * y + 96].astype(BF16)
 
@@ -1401,6 +1420,7 @@
     to_f, to_q, to_v = (2 * slim, 384), (96, 128), (32, 128)
     scratch += [pltpu.VMEM((2, 2) + k, BF16) for k in (to_f, to_f, to_q, to_q, to_v)]
     scratch += [pltpu.VMEM((4,) + k, BF16) for k in (to_f, to_f, to_q, to_q, to_v)]
+    scratch += [pltpu.VMEM((2, 3, 256, 128), BF16)]
     scratch += [pltpu.SemaphoreType.DMA((n, 8)), pltpu.SemaphoreType.DMA((3,)), pltpu.SemaphoreType.DMA((24,)), pltpu.SemaphoreType.DMA((24,))]
     scratch += shares[0].scratch(p)
     for s in shares[1:]:

time: 155 us -> 154 us (level)
  no operation moved by 1% of the time
where the time goes in v4:
time: 154 us; the launch traced here: 153 us
  Pallas kernels  152 us (99%)
    pallas_call x1, Pallas kernels, front(): pl.pallas_call(functools.partial(front_kernel, p, owned), out_shape=[act(...  81.1 us
    pallas_call x1, Pallas kernels, closing_owned(): pl.pallas_call(functools.partial(owner_kernel, p, shares), out_shape=outs...  67.7 us
    pallas_call x1, Pallas kernels, hand_over(): pl.pallas_call(functools.partial(hand_over_kernel, count), out_shape=[jax...  3.63 us

profile of v4, /device:TPU:0, one launch (start us, length us, event | category | flops | bytes accessed | tf_op | source)
XLA Modules:
  0.0 153.3 jit_solution(9317044822314305425)
XLA Ops:
  0.6 81.1 %shard_map.237 = (bf16[2,768,512]{2,1,0:T(8,128)(2,1)}, bf16[2,512,768]{2,1,0:T(8,128)(2,1)}, bf16[2,768,512]{2,1,0:T(8,128)(2,1)}, bf16[2,512,768]{2,1,0:T(8,12...) custom-call(s32[2,4]{1,0:T(2,128)} %refs_0_.1, ...), custom_call_target="tpu_custom_call" | custom-call | tf_op jit(solution)/shard_map/pallas_call | solution.py:641
  81.7 67.7 %shard_map.238 = (bf16[2,512,768]{2,1,0:T(8,128)(2,1)}, f32[12,24,48]{2,1,0:T(8,128)}, f32[1,192,96]{2,1,0:T(8,128)}, f32[4,24,192]{2,1,0:T(8,128)}, f32[4,24,19...) custom-call(s32[2,4]{1,0:T(2,128)} %refs_0_.1, ...), custom_call_target="tpu_custom_call" | custom-call | tf_op jit(solution)/shard_map/pallas_call | solution.py:1428
  149.4 3.6 %shard_map.239 = (bf16[2,512,768]{2,1,0:T(8,128)(2,1)}, bf16[2,512,768]{2,1,0:T(8,128)(2,1)}, f32[12,24,48]{2,1,0:T(8,128)}, f32[1,192,96]{2,1,0:T(8,128)}, f32[...) custom-call(bf16[2,512,768]{2,1,0:T(8,128)(2,1)} %get-tuple-element., ...), custom_call_target="tpu_custom_call" | custom-call | tf_op jit(solution)/shard_map/pallas_call | solution.py:1455
